TPU v7x, 32 devices: a whole 2x2x4 slice. The times are simulated.
32 devices in a mesh: groups: 2 (over y), strip: 4 (over z), section: 2 (over x), col: 2 (over core).
Axes of the slice: x: 2, y: 2, z: 4, core: 2. Of those that a mesh axis runs over, the one named last changes fastest.
Arguments:
- x_in: float32 [8, 512, 16, 256], P('groups', None, 'strip', 'col'), parts along dimension 0, may hold values from -6 to 6
- w_reduce: float32 [2, 128, 512], P('section'), may hold values from -0.25 to 0.25
- w_spatial: float32 [2, 9, 128, 128], P('section'), may hold values from -0.1875 to 0.1875
- w_expand: float32 [2, 512, 128], P('section'), may hold values from -0.5 to 0.5
- gain_mid: float32 [2, 2, 128], P('section'), may hold values from 0.1 to 1.9
- bias_mid: float32 [2, 2, 128], P('section'), may hold values from -3 to 3
- gain_out: float32 [2, 512], P('section'), may hold values from 0.1 to 1.9
- bias_out: float32 [2, 512], P('section'), may hold values from -3 to 3
Outputs:
- features: float32 [2, 8, 512, 16, 256], P('section', 'groups', None, 'strip', 'col'), parts along dimension 1
There are 2 independent parts, one for each index of `groups`. A program takes and returns all parts, laid end to end along the dimension named above; an argument that names none is the same for every part. Nothing has to cross between parts.
All inputs are finite; a program needn't handle non-finite values.
Results may differ from a plain program's by a relative error of at most 0.00015.
Values sent between devices are 32-bit elements; how exact they have to be, the bound alone decides.
No kernel may reach another device: no remote copies, remote signals or barrier semaphores. Data moves between devices by JAX's collectives and lax.ppermute only.
A program may use at most 64 MiB of HBM per device.

v0:
```python
import functools

import jax
import jax.numpy as jnp
from jax import lax
from jax.experimental import pallas as pl
from jax.experimental.pallas import tpu as pltpu
from jax.sharding import PartitionSpec as P

F32 = jnp.float32
BF16 = jnp.bfloat16
PAD = 8


def split(value):
    high = value.astype(BF16)
    return high, (value - high.astype(F32)).astype(BF16)


def dot(left, right):
    return jnp.dot(left, right, preferred_element_type=F32)


def dot_nt(left, right):
    return lax.dot_general(left, right, (((1,), (1,)), ((), ())), preferred_element_type=F32)


def first_core():
    return lax.axis_index("col") == 0


def even_strip():
    return lax.axis_index("strip") % 2 == 0


def column_of(row):
    return jnp.concatenate(
        [
            jnp.transpose(jnp.broadcast_to(row[:, at : at + 128], (128, 128)))
            for at in range(0, row.shape[1], 128)
        ],
        axis=0,
    )


def pack_first_kernel(
    w_reduce, gain_mid, bias_mid, gain_out, bias_out, first, gain_held, bias_held, gain_row, bias_row, sem
):
    half = w_reduce.shape[1] // 2
    cm = gain_mid.shape[2]
    start = pl.multiple_of(lax.axis_index("col") * half, half)
    moves = [
        (w_reduce.at[0, pl.ds(start, half), :], first.at[:half, :]),
        (gain_mid.at[0], gain_held),
        (bias_mid.at[0], bias_held),
        (gain_out, gain_row),
        (bias_out, bias_row),
    ]
    copies = [pltpu.make_async_copy(here, there, sem.at[i]) for i, (here, there) in enumerate(moves)]
    for copy in copies:
        copy.start()
    first[half : half + 8, :] = jnp.zeros((8, first.shape[1]), F32)
    for copy in copies:
        copy.wait()
    for i in range(2):
        first[half : half + 1, i * cm : (i + 1) * cm] = gain_held[i : i + 1, :]
        first[half : half + 1, (2 + i) * cm : (3 + i) * cm] = bias_held[i : i + 1, :]
    first[half + 1 : half + 2, :] = gain_row[...]
    first[half + 2 : half + 3, :] = bias_row[...]


def pack_rest_kernel(w_spatial, w_expand, rest, sem):
    half = w_spatial.shape[2] // 2
    wide = w_expand.shape[1] // 2
    low = pl.multiple_of(lax.axis_index("col") * half, half)
    at = pl.multiple_of(lax.axis_index("col") * wide, wide)
    copies = [
        pltpu.make_async_copy(
            w_spatial.at[0, tap, pl.ds(low, half), :], rest.at[tap * half : (tap + 1) * half, :], sem.at[tap]
        )
        for tap in range(9)
    ]
    copies.append(
        pltpu.make_async_copy(w_expand.at[0, pl.ds(at, wide), :], rest.at[9 * half :, :], sem.at[9])
    )
    for copy in copies:
        copy.start()
    for copy in copies:
        copy.wait()


def fetch_kernel(x, held, sem):
    copies = [pltpu.make_async_copy(x.at[t], held.at[t], sem.at[t]) for t in range(x.shape[0])]
    for copy in copies:
        copy.start()
    for copy in copies:
        copy.wait()


def store_reduce(w_high, at, rows):
    cm = w_high.shape[0] // 2
    high, low = split(rows)
    w_high[at : at + rows.shape[0], :] = high
    w_high[cm + at : cm + at + rows.shape[0], :] = low


def store_rest(tap_rows, expand_rows, gain_out, w_spatial, w_expand):
    cm = w_expand.shape[1] // 3
    for tap in range(9):
        high, low = split(jnp.transpose(tap_rows(tap)))
        w_spatial[tap * cm : (tap + 1) * cm, :cm] = high
        w_spatial[tap * cm : (tap + 1) * cm, cm:] = low
    high, low = split(expand_rows * column_of(gain_out))
    w_expand[:, :cm] = high
    w_expand[:, cm : 2 * cm] = low
    w_expand[:, 2 * cm :] = high


def prepare_own_kernel(w_reduce, w_spatial, w_expand, first, out_reduce, out_spatial, out_expand, out_shift, out_terms):
    half = w_reduce.shape[1] // 2
    store_reduce(out_reduce, 0, w_reduce[0])
    terms = first[half : half + 8, :]
    out_terms[...] = terms
    out_shift[...] = column_of(terms[2:3, :])
    store_rest(lambda tap: w_spatial[0, tap], w_expand[0], terms[1:2, :], out_spatial, out_expand)


def prepare_reduce_kernel(level, mine, other, own_reduce, own_terms, out_reduce, out_terms):
    half = mine.shape[0] - 8

    @pl.when(lax.axis_index("section") == level)
    def _():
        out_reduce[...] = own_reduce[...]
        out_terms[...] = own_terms[...]

    @pl.when(lax.axis_index("section") != level)
    def _():
        out_terms[...] = mine[half:, :]
        for core in range(2):

            @pl.when(lax.axis_index("col") == core)
            def _(core=core):
                store_reduce(out_reduce, core * half, mine[:half, :])
                store_reduce(out_reduce, (1 - core) * half, other[:half, :])


def prepare_rest_kernel(
    level, mine, other, terms, own_spatial, own_expand, own_shift, out_spatial, out_expand, out_shift
):
    cm = own_expand.shape[1] // 3
    half, wide = cm // 2, own_expand.shape[0] // 2

    @pl.when(lax.axis_index("section") == level)
    def _():
        out_spatial[...] = own_spatial[...]
        out_expand[...] = own_expand[...]
        out_shift[...] = own_shift[...]

    @pl.when(lax.axis_index("section") != level)
    def _():
        out_shift[...] = column_of(terms[2:3, :])
        for core in range(2):

            @pl.when(lax.axis_index("col") == core)
            def _(core=core):
                low, up = (mine, other) if core == 0 else (other, mine)

                def tap_rows(tap):
                    at = slice(tap * half, (tap + 1) * half)
                    return jnp.concatenate([low[at, :], up[at, :]], axis=0)

                expand = jnp.concatenate([low[9 * half :, :], up[9 * half :, :]], axis=0)
                store_rest(tap_rows, expand, terms[1:2, :], out_spatial, out_expand)


def members(kind, rows):
    return (0, rows - 1) if kind == "border" else tuple(range(1, rows - 1))


def reduce_step(tile, field, w_reduce, terms, r_out, edge, msgs):
    cm = w_reduce.shape[0] // 2
    count, cols = r_out.shape[1:3]
    high, low = split(field)
    both = dot(w_reduce[...], high)
    total = both[:cm] + both[cm:] + dot(w_reduce[:cm, :], low)
    gain, shift = terms[0:1, 0:cm], terms[0:1, 2 * cm : 3 * cm]
    even, first = even_strip(), first_core()
    turned = []
    for j in range(count):
        part = jnp.maximum(jnp.transpose(total[:, j * cols : (j + 1) * cols]) * gain + shift, 0.0)
        r_out[tile, j] = part
        at = tile * count + j
        edge[at : at + 1, :] = jnp.where(first, part[cols - 1 : cols, :], part[0:1, :])
        turned.append(part)
    if msgs:
        msgs[0][tile] = jnp.where(even, turned[-1], turned[0])
        msgs[1][tile] = jnp.where(even, turned[0], turned[-1])


def field_rows(x, kind, rows, tile, j):
    if len(x.shape) == 3:
        return x[tile, pl.ds(members(kind, rows)[j], x.shape[1] // rows, stride=rows), :]
    return x[tile, j]


def bring(x, held, sem, start):
    copies = [pltpu.make_async_copy(x.at[t], held.at[t], sem.at[t]) for t in range(x.shape[0])]
    if start:
        for copy in copies:
            copy.start()
    return copies


def reduce_kernel(kind, rows, x, w_reduce, terms, r_out, edge, *refs):
    msgs, copies = refs, None
    if kind == "inner":
        msgs = ()
        copies = bring(x, *refs, True)
        x = refs[0]
    edge[...] = jnp.zeros_like(edge)
    count = r_out.shape[1]
    for tile in range(x.shape[0]):
        if copies:
            copies[tile].wait()
        field = jnp.concatenate([field_rows(x, kind, rows, tile, j) for j in range(count)], axis=1)
        reduce_step(tile, field, w_reduce, terms, r_out, edge, msgs)


def block_kernel(kind, rows, level, last, *refs):
    refs = list(refs)

    def take(n):
        taken, refs[:n] = refs[:n], []
        return taken

    border = kind == "border"
    x, r_border, r_inner, edge_border, edge_inner = take(5)
    if border:
        halo_a, halo_b, corners = take(3)
    w_spatial, w_expand, shift_out, terms = take(4)
    if not last:
        next_reduce, next_terms = take(2)
    if last and border:
        take(1)
    else:
        take(1)
    outs = take(2 if last and border else 1)
    if not last:
        r_out, edge_out = take(2)
        msgs = take(2) if border else []
        edge_out[...] = jnp.zeros_like(edge_out)
    padded, taps_high, taps_low = take(3)
    copies = None
    if len(x.shape) == 3:
        x_held, x_sem = take(2)
        copies = bring(x, x_held, x_sem, True)
        x = x_held
    tiles, _, cols, cm = r_border.shape
    chosen = members(kind, rows)
    count = len(chosen)
    inner = members("inner", rows)
    even, first = even_strip(), first_core()
    gain, shift = terms[0:1, cm : 2 * cm], terms[0:1, 3 * cm : 4 * cm]
    keep = lax.axis_index("section") >= level

    def row_and_side(tile, i):
        if i in (-1, rows):
            from_a = even if i == rows else jnp.logical_not(even)
            side_a, side_b = corners[tile : tile + 1, :], corners[tiles + tile : tiles + tile + 1, :]
            return jnp.where(from_a, halo_a[tile], halo_b[tile]), jnp.where(from_a, side_a, side_b)
        if i in (0, rows - 1):
            j = 0 if i == 0 else 1
            return r_border[tile, j], edge_border[2 * tile + j : 2 * tile + j + 1, :]
        j = inner.index(i)
        at = tile * len(inner) + j
        return r_inner[tile, j], edge_inner[at : at + 1, :]

    span = count * cols
    for tile in range(tiles):
        for i in sorted({r + p for r in chosen for p in (-1, 0, 1)}):
            field, side = row_and_side(tile, i)
            slot = padded.at[tile, i + 1]
            slot[PAD : PAD + cols, :] = field
            slot[PAD - 1 : PAD, :] = jnp.where(first, 0.0, side)
            slot[PAD + cols : PAD + cols + 1, :] = jnp.where(first, side, 0.0)
            for q in range(3):
                high, low = split(field if q == 1 else slot[PAD - 1 + q : PAD - 1 + q + cols, :])
                for j, r in enumerate(chosen):
                    p = i - r + 1
                    if 0 <= p <= 2:
                        lanes = slice((3 * p + q) * cm, (3 * p + q + 1) * cm)
                        at = (tile * count + j) * cols
                        taps_high[at : at + cols, lanes] = high
                        taps_low[at : at + cols, lanes] = low
    group = 4
    middles = []
    for g in range(0, tiles, group):
        at = slice(g * span, (g + group) * span)
        both = dot(taps_high[at, :], w_spatial[...])
        spatial = both[:, :cm] + both[:, cm:] + dot(taps_low[at, :], w_spatial[:, :cm])
        high, low = split(jnp.maximum(spatial * gain + shift, 0.0))
        middles.append(jnp.concatenate([high, high, low], axis=1))
    for tile in range(tiles):
        g, k = tile // group, tile % group
        branch = dot_nt(w_expand[...], middles[g][k * span : (k + 1) * span])
        after = []
        if copies:
            copies[tile].wait()
        for j in range(count):
            before = field_rows(x, kind, rows, tile, j)
            new = jnp.maximum(before + branch[:, j * cols : (j + 1) * cols] + shift_out[...], 0.0)
            after.append(jnp.where(keep, new, before))
            if last:
                whole = outs[-1]
                whole[tile, pl.ds(chosen[j], whole.shape[1] // rows, stride=rows), :] = after[j]
            else:
                outs[0][tile, j] = after[j]
        if not last:
            field = jnp.concatenate(after, axis=1)
            reduce_step(tile, field, next_reduce, next_terms, r_out, edge_out, msgs)
        if last and border:
            sem = refs[0]
            pltpu.make_async_copy(outs[1].at[tile], outs[0].at[tile], sem.at[tile]).start()
    if last and border:
        sem = refs[0]
        for tile in range(tiles):
            pltpu.make_async_copy(outs[1].at[tile], outs[0].at[tile], sem.at[tile]).wait()


VMEM = pl.BlockSpec(memory_space=pltpu.VMEM)
ANY = pl.BlockSpec(memory_space=pl.ANY)
HBM = pl.BlockSpec(memory_space=pl.ANY)
FAR = pl.BlockSpec(memory_space=pltpu.VMEM)


def near(shape, dtype=F32):
    return pltpu.VMEM(shape, dtype)


def call(kernel, name, args, outs, scratch=(), flops=0, moved=0, specs=None, out_specs=None, aliases=None):
    held = {id(VMEM): pltpu.VMEM, id(HBM): pltpu.HBM, id(FAR): pltpu.HBM}
    arrays = [pltpu.with_memory_space_constraint(a, held[id(s)]) if id(s) in held else a for a, s in args]
    return pl.pallas_call(
        kernel,
        name=name,
        in_specs=[spec for _, spec in args],
        out_specs=out_specs or [VMEM] * len(outs),
        out_shape=outs,
        scratch_shapes=list(scratch),
        input_output_aliases=aliases or {},
        compiler_params=pltpu.CompilerParams(vmem_limit_bytes=24 * 2**20),
        cost_estimate=pl.CostEstimate(flops=flops, bytes_accessed=moved, transcendentals=0),
    )(*arrays)


def on_device(x_in, w_reduce, w_spatial, w_expand, gain_mid, bias_mid, gain_out, bias_out):
    sections = lax.axis_size("section")
    strips = lax.axis_size("strip")
    section = lax.axis_index("section")
    strip = lax.axis_index("strip")
    core = lax.axis_index("col")
    tiles, c, rows, cols = x_in.shape
    cm = w_reduce.shape[1]
    half, wide = cm // 2, c // 2
    inner = rows - 2
    cells = tiles * rows * cols

    def swap(array):
        return lax.ppermute(array, "col", [(0, 1), (1, 0)])

    def from_section(array, level):
        total = None
        for step in range(1, sections - level):
            sent = lax.ppermute(array, "section", [(i, i + step) for i in range(sections - step)])
            total = sent if total is None else jnp.where(section - level == step, sent, total)
        return total

    def pairs(start):
        found = []
        for i in range(start, strips - 1, 2):
            found += [(i, i + 1), (i + 1, i)]
        return found

    (first,) = call(
        pack_first_kernel, "pack_first",
        [(a, HBM) for a in (w_reduce, gain_mid, bias_mid, gain_out, bias_out)],
        [near((half + 8, c))],
        [pltpu.VMEM((2, cm), F32)] * 2 + [pltpu.VMEM((1, c), F32)] * 2 + [pltpu.SemaphoreType.DMA((5,))],
        moved=4 * half * c,
    )
    first_sent = [from_section(first, level) for level in range(sections - 1)]
    (rest,) = call(
        pack_rest_kernel, "pack_rest", [(w_spatial, HBM), (w_expand, HBM)],
        [near((9 * half + wide, cm))], [pltpu.SemaphoreType.DMA((10,))], moved=4 * (9 * half + wide) * cm,
    )
    rest_sent = [from_section(rest, level) for level in range(sections - 1)]
    flat = x_in.reshape(tiles, c * rows, cols)
    (held,) = call(
        fetch_kernel, "fetch", [(flat, HBM)], [near(flat.shape)], [pltpu.SemaphoreType.DMA((tiles,))],
        moved=4 * cells * c,
    )
    rest_shapes = [near((9 * cm, 2 * cm), BF16), near((c, 3 * cm), BF16), near((c, 128))]
    own_reduce, own_spatial, own_expand, own_shift, own_terms = call(
        prepare_own_kernel, "prepare_own", [(w_reduce, FAR), (w_spatial, FAR), (w_expand, FAR), (first, VMEM)],
        [near((2 * cm, c), BF16)] + rest_shapes + [near((8, c))], moved=4 * cm * (2 * c + 9 * cm),
    )

    first_sent, held, _ = lax.optimization_barrier((first_sent, held, own_reduce))

    def reduce_weights(level):
        if level == sections - 1:
            return own_reduce, own_terms
        mine = first_sent[level]
        return call(
            functools.partial(prepare_reduce_kernel, level), "prepare_reduce",
            [(a, VMEM) for a in (mine, swap(mine), own_reduce, own_terms)],
            [near((2 * cm, c), BF16), near((8, c))], moved=4 * cm * c,
        )

    def rest_weights(level, terms):
        if level == sections - 1:
            return own_spatial, own_expand, own_shift
        mine = rest_sent[level]
        return call(
            functools.partial(prepare_rest_kernel, level), "prepare_rest",
            [(a, VMEM) for a in (mine, swap(mine), terms, own_spatial, own_expand, own_shift)],
            rest_shapes, moved=4 * cm * (c + 9 * cm),
        )

    def reduced_shapes(kind):
        count = 2 if kind == "border" else inner
        shapes = [near((tiles, count, cols, cm)), near((-(-tiles * count // 8) * 8, cm))]
        return shapes + ([near((tiles, cols, cm))] * 2 if kind == "border" else [])

    def reduce_call(kind, level, weights):
        return call(
            functools.partial(reduce_kernel, kind, rows), "reduce_" + kind,
            [(held, VMEM) if kind == "border" else (flat, HBM)] + [(a, VMEM) for a in weights],
            reduced_shapes(kind), [] if kind == "border" else tile_scratch, flops=3 * cells * c * cm, moved=4 * cells * c // 2,
        )

    tile_scratch = [pltpu.VMEM(flat.shape, F32), pltpu.SemaphoreType.DMA((tiles,))]

    def scratch(kind):
        count = 2 if kind == "border" else inner
        return [
            pltpu.VMEM((tiles, rows + 2, cols + 2 * PAD, cm), F32),
            pltpu.VMEM((tiles * count * cols, 9 * cm), BF16),
            pltpu.VMEM((tiles * count * cols, 9 * cm), BF16),
        ]

    def halos(msg_a, msg_b):
        halo_a = lax.ppermute(msg_a, "strip", pairs(0))
        halo_b = lax.ppermute(msg_b, "strip", pairs(1))
        at = jnp.where(core == 0, cols - 1, 0)
        edge_a = lax.dynamic_slice_in_dim(halo_a, at, 1, 1)
        edge_b = lax.dynamic_slice_in_dim(halo_b, at, 1, 1)
        return halo_a, halo_b, swap(jnp.concatenate([edge_a[:, 0], edge_b[:, 0]], axis=0))

    def block_call(kind, level, x, sent, weights, next_weights, before, halo=None):
        last = level == sections - 1
        (r_border, edge_border), (r_inner, edge_inner) = sent
        args = [(x, HBM if x is flat else VMEM)]
        args += [(a, VMEM) for a in (r_border, r_inner, edge_border, edge_inner)]
        if kind == "border":
            args += [(a, VMEM) for a in halo]
        args += [(a, VMEM) for a in weights]
        if not last:
            args += [(a, VMEM) for a in next_weights]
        args.append((before, VMEM if last and kind == "border" else ANY))
        count = 2 if kind == "border" else inner
        more, out_specs, aliases, held_out = scratch(kind), None, None, near((tiles, count, c, cols))
        if x is flat:
            more += tile_scratch
        if last:
            held_out = near(flat.shape)
        outs = [held_out] + ([] if last else reduced_shapes(kind))
        if last and kind == "border":
            outs = [pltpu.HBM(flat.shape, F32), held_out]
            out_specs = [ANY, VMEM]
            aliases = {len(args) - 1: 1}
            more.append(pltpu.SemaphoreType.DMA((tiles,)))
        return call(
            functools.partial(block_kernel, kind, rows, level, last), "block_" + kind, args, outs, more,
            flops=3 * cells * (13 if last else 17) * cm * cm, moved=4 * cells * c, out_specs=out_specs, aliases=aliases,
        )

    weights = reduce_weights(0)
    border = reduce_call("border", 0, weights)
    halo = halos(border[2], border[3])
    inside = reduce_call("inner", 0, weights)
    x_border = x_inner = flat
    for level in range(sections):
        last = level == sections - 1
        terms = weights[1]
        rest_of = tuple(rest_weights(level, terms)) + (terms,)
        sent = ((border[0], swap(border[1])), (inside[0], swap(inside[1])))
        if last:
            (part,) = block_call("inner", level, x_inner, sent, rest_of, None, first)
            whole = block_call("border", level, x_border, sent, rest_of, None, part, halo)[0]
        else:
            weights = reduce_weights(level + 1)
            x_border, *border = block_call("border", level, x_border, sent, rest_of, weights, first, halo)
            halo = halos(border[2], border[3])
            x_inner, *inside = block_call("inner", level, x_inner, sent, rest_of, weights, x_border)
    return whole.reshape(1, tiles, c, rows, cols)


def solution(mesh):
    in_specs = (
        P("groups", None, "strip", "col"),
        P("section", None, None),
        P("section", None, None, None),
        P("section", None, None),
        P("section", None, None),
        P("section", None, None),
        P("section", None),
        P("section", None),
    )
    out_specs = P("section", "groups", None, "strip", "col")
    return jax.shard_map(
        on_device, mesh=mesh, in_specs=in_specs, out_specs=out_specs, check_vma=False
    )
```

profile of v0, /device:TPU:17, one launch (start us, length us, event | category | flops | bytes accessed | tf_op | source)
XLA Modules:
  0.0 51.3 jit_solution(281144567131450685)
XLA Ops:
  0.0 1.0 %pack_first.1.first.refs_14_.refs_9_ = f32[72,512]{1,0:T(8,128)S(1)} custom-call(f32[1,128,512]{2,1,0:T(8,128)} %w_reduce.3, f32[1,2,128]{2,1,0:T(2,128)} %gain_mid.1, f32[1,2,128]{2,1,0:T(2,128)} %bias_mid.1, f32[1,512]{1,0:T(1,128)} %gain_out.1, f32[1,512]{1,0:T(1,128)} %bias_out.1), custom_call_target="tpu_custom_call" | custom-call | bytes 131072 | tf_op jit(solution)/shard_map/pack_first/pallas_call | solution.py:343
  1.0 3.1 %collective-permute-start = (f32[72,512]{1,0:T(8,128)S(1)}, f32[72,512]{1,0:T(8,128)S(1)}, u32[]{:S(2)}, u32[]{:S(2)}) collective-permute-start(f32[72,512]{1,0:T(8,128)S(1)} %pack_first.1.first.refs_14_.refs_9_), channel_id=1, source_target_pairs={{0,2},{1,3},{4,6},{5,7},{8,10},{9,11},{12,14},{13,15},{16,18},{17,... | collective-permute-start | bytes 442376 | tf_op jit(solution)/shard_map/ppermute | solution.py:374
  4.1 1.2 %pack_rest.1 = f32[832,128]{1,0:T(8,128)S(1)} custom-call(f32[1,9,128,128]{3,2,1,0:T(8,128)} %w_spatial.3, f32[1,512,128]{2,1,0:T(8,128)} %w_expand.3), custom_call_target="tpu_custom_call" | custom-call | bytes 425984 | tf_op jit(solution)/shard_map/pack_rest/pallas_call | solution.py:343
  5.3 1.3 %collective-permute-start.7 = (f32[832,128]{1,0:T(8,128)S(1)}, f32[832,128]{1,0:T(8,128)S(1)}, u32[]{:S(2)}, u32[]{:S(2)}) collective-permute-start(f32[832,128]{1,0:T(8,128)S(1)} %pack_rest.1), channel_id=1, source_target_pairs={{0,2},{1,3},{4,6},{5,7},{8,10},{9,11},{12,14},{13,15},{16,18},{17,... | collective-permute-start | bytes 1277960 | tf_op jit(solution)/shard_map/ppermute | solution.py:374
  6.6 1.6 %prepare_own.1 = (bf16[256,512]{1,0:T(8,128)(2,1)S(1)}, bf16[1152,256]{1,0:T(8,128)(2,1)S(1)}, bf16[512,384]{1,0:T(8,128)(2,1)S(1)}, f32[512,128]{1,0:T(8,128)S(1)}, f32[8,512]{1,0:T(8,128)S(1)}) custom-call(f32[1,128,512]{2,1,0:T(8,128)} %w_reduce.3, f32[1,9,128,128]{3,2,1,0:T(8,128)} %w_spatial.3, f32[1,512,128]{2,1,0:T(8,128)} %w_expand.3, ...), custom_call_target="tpu_custom_call" | custom-call | bytes 1114112 | tf_op jit(solution)/shard_map/prepare_own/pallas_call | solution.py:343
  8.2 2.2 %fetch.1.x = f32[4,2048,128]{2,1,0:T(8,128)S(1)} custom-call(f32[4,2048,128]{2,1,0:T(8,128)} %bitcast.6), custom_call_target="tpu_custom_call" | custom-call | bytes 4194304 | tf_op jit(solution)/shard_map/fetch/pallas_call | solution.py:343
  10.4 0.0 collective-permute-done.mine
  10.4 1.0 %collective-permute-start.1 = (f32[72,512]{1,0:T(8,128)S(1)}, f32[72,512]{1,0:T(8,128)S(1)}, u32[]{:S(2)}, u32[]{:S(2)}) collective-permute-start(f32[72,512]{1,0:T(8,128)S(1)} %collective-permute-done.mine), channel_id=1, source_target_pairs={{0,1},{1,0},{2,3},{3,2},{4,5},{5,4},{6,7},{7,6},{8,9},{9,8},{10,11... | collective-permute-start | bytes 442376 | tf_op jit(solution)/shard_map/ppermute | solution.py:369
  11.5 1.0 %collective-permute-done.1.other = f32[72,512]{1,0:T(8,128)S(1)} collective-permute-done((f32[72,512]{1,0:T(8,128)S(1)}, f32[72,512]{1,0:T(8,128)S(1)}, u32[]{:S(2)}, u32[]{:S(2)}) %collective-permute-start.1) | collective-permute-done | bytes 147488 | tf_op jit(solution)/shard_map/ppermute | solution.py:369
  12.5 1.5 %reduce_border.1 = (f32[4,2,128,128]{3,2,1,0:T(8,128)S(1)}, f32[8,128]{1,0:T(8,128)S(1)}, f32[4,128,128]{2,1,0:T(8,128)}, f32[4,128,128]{2,1,0:T(8,128)}) custom-call(f32[4,2048,128]{2,1,0:T(8,128)S(1)} %fetch.1.x, bf16[256,512]{1,0:T(8,128)(2,1)S(1)} %get-tuple-element.36.w_reduce, f32[8,512]{1,0:T(8,128)S(1)} %get-tuple-element.37.terms.refs_11_.refs_8_), custom_call_target="tpu_custom_call" | custom-call | flops 402653184 | bytes 2097152 | tf_op jit(solution)/shard_map/reduce_border/pallas_call | solution.py:343
  14.0 1.3 %collective-permute-start.4 = (f32[4,128,128]{2,1,0:T(8,128)}, f32[4,128,128]{2,1,0:T(8,128)}, u32[]{:S(2)}, u32[]{:S(2)}) collective-permute-start(f32[4,128,128]{2,1,0:T(8,128)} %get-tuple-element.42), channel_id=1, source_target_pairs={{0,4},{4,0},{8,12},{12,8},{1,5},{5,1},{9,13},{13,9},{2,6},{6,2},{1... | collective-permute-start | bytes 786440 | tf_op jit(solution)/shard_map/ppermute | solution.py:453
  15.3 1.9 %collective-permute-start.5 = (f32[4,128,128]{2,1,0:T(8,128)}, f32[4,128,128]{2,1,0:T(8,128)}, u32[]{:S(2)}, u32[]{:S(2)}) collective-permute-start(f32[4,128,128]{2,1,0:T(8,128)} %get-tuple-element.43), channel_id=1, source_target_pairs={{4,8},{8,4},{5,9},{9,5},{6,10},{10,6},{7,11},{11,7},{20,24},{24,20... | collective-permute-start | bytes 786440 | tf_op jit(solution)/shard_map/ppermute | solution.py:454
  17.2 0.0 collective-permute-done.7.mine
  17.2 0.7 %collective-permute-start.8 = (f32[832,128]{1,0:T(8,128)S(1)}, f32[832,128]{1,0:T(8,128)S(1)}, u32[]{:S(2)}, u32[]{:S(2)}) collective-permute-start(f32[832,128]{1,0:T(8,128)S(1)} %collective-permute-done.7.mine), channel_id=1, source_target_pairs={{0,1},{1,0},{2,3},{3,2},{4,5},{5,4},{6,7},{7,6},{8,9},{9,8},{10,11... | collective-permute-start | bytes 1277960 | tf_op jit(solution)/shard_map/ppermute | solution.py:369
  17.9 0.1 collective-permute-start.2
  18.0 3.0 %reduce_inner.1 = (f32[4,2,128,128]{3,2,1,0:T(8,128)S(1)}, f32[8,128]{1,0:T(8,128)S(1)}) custom-call(f32[4,2048,128]{2,1,0:T(8,128)} %bitcast.7, bf16[256,512]{1,0:T(8,128)(2,1)S(1)} %get-tuple-element.36.w_reduce, f32[8,512]{1,0:T(8,128)S(1)} %get-tuple-element.37.terms.refs_11_.refs_8_), custom_call_target="tpu_custom_call" | custom-call | flops 402653184 | bytes 2097152 | tf_op jit(solution)/shard_map/reduce_inner/pallas_call | solution.py:343
  21.0 0.5 collective-permute-start.3
  21.5 0.4 collective-permute-done.4.refs_5_
  21.8 0.7 %constant_dynamic-slice_fusion.3 = f32[4,1,128]{2,1,0:T(1,128)S(1)} fusion(f32[4,128,128]{2,1,0:T(8,128)} %collective-permute-done.4.refs_5_, s32[]{:T(128)S(6)} %select_n.5), kind=kLoop, calls=%fused_computation.5 | loop fusion | bytes 4100 | tf_op jit(solution)/shard_map/dynamic_slice | solution.py:456
  22.6 2.1 %collective-permute-done.5.refs_6_ = f32[4,128,128]{2,1,0:T(8,128)} collective-permute-done((f32[4,128,128]{2,1,0:T(8,128)}, f32[4,128,128]{2,1,0:T(8,128)}, u32[]{:S(2)}, u32[]{:S(2)}) %collective-permute-start.5) | collective-permute-done | bytes 262176 | tf_op jit(solution)/shard_map/ppermute | solution.py:454
  24.7 0.7 %constant_dynamic-slice_fusion.2 = f32[4,1,128]{2,1,0:T(1,128)S(1)} fusion(f32[4,128,128]{2,1,0:T(8,128)} %collective-permute-done.5.refs_6_, s32[]{:T(128)S(6)} %select_n.5), kind=kLoop, calls=%fused_computation.4 | loop fusion | bytes 4100 | tf_op jit(solution)/shard_map/dynamic_slice | solution.py:457
  25.4 1.6 %collective-permute-start.6 = (f32[8,128]{1,0:T(8,128)S(1)}, f32[8,128]{1,0:T(8,128)S(1)}, u32[]{:S(2)}, u32[]{:S(2)}) collective-permute-start(f32[8,128]{1,0:T(8,128)S(1)} %pad_maximum_fusion), channel_id=1, source_target_pairs={{0,1},{1,0},{2,3},{3,2},{4,5},{5,4},{6,7},{7,6},{8,9},{9,8},{10,11... | collective-permute-start | bytes 12296 | tf_op jit(solution)/shard_map/ppermute | solution.py:369
  27.0 0.0 collective-permute-done.8.other
  27.0 0.1 prepare_rest.1
  27.1 0.0 collective-permute-done.2.refs_3_
  27.1 0.0 collective-permute-done.3.refs_4_
  27.1 0.7 %collective-permute-done.6.refs_7_ = f32[8,128]{1,0:T(8,128)S(1)} collective-permute-done((f32[8,128]{1,0:T(8,128)S(1)}, f32[8,128]{1,0:T(8,128)S(1)}, u32[]{:S(2)}, u32[]{:S(2)}) %collective-permute-start.6) | collective-permute-done | bytes 4128 | tf_op jit(solution)/shard_map/ppermute | solution.py:369
  27.8 5.6 %block_border.2 = (f32[4,2,512,128]{3,2,1,0:T(8,128)S(1)}, f32[4,2,128,128]{3,2,1,0:T(8,128)S(1)}, f32[8,128]{1,0:T(8,128)S(1)}, f32[4,128,128]{2,1,0:T(8,128)S(1)}, f32[4,128,128]{2,1,0:T(8,128)S(1)}) custom-call(f32[4,2048,128]{2,1,0:T(8,128)} %bitcast.8, f32[4,2,128,128]{3,2,1,0:T(8,128)S(1)} %get-tuple-element.38.refs_1_, ...), custom_call_target="tpu_custom_call" | custom-call | flops 1711276032 | bytes 4194304 | tf_op jit(solution)/shard_map/block_border/pallas_call | solution.py:343
  33.4 0.1 collective-permute-start.11
  33.5 0.4 collective-permute-start.9
  33.9 2.1 %collective-permute-start.12 = (f32[4,128,128]{2,1,0:T(8,128)S(1)}, f32[4,128,128]{2,1,0:T(8,128)S(1)}, u32[]{:S(2)}, u32[]{:S(2)}) collective-permute-start(f32[4,128,128]{2,1,0:T(8,128)S(1)} %get-tuple-element.56), channel_id=1, source_target_pairs={{4,8},{8,4},{5,9},{9,5},{6,10},{10,6},{7,11},{11,7},{20,24},{24,20... | collective-permute-start | bytes 786440 | tf_op jit(solution)/shard_map/ppermute | solution.py:454
  36.0 4.5 %block_inner.2 = (f32[4,2,512,128]{3,2,1,0:T(8,128)S(1)}, f32[4,2,128,128]{3,2,1,0:T(8,128)S(1)}, f32[8,128]{1,0:T(8,128)S(1)}) custom-call(f32[4,2048,128]{2,1,0:T(8,128)} %bitcast.9, f32[4,2,128,128]{3,2,1,0:T(8,128)S(1)} %get-tuple-element.38.refs_1_, f32[4,2,128,128]{3,2,1,0:T(8,128)S(1)} %get-tuple-element.39.refs_2_, ...), custom_call_target="tpu_custom_call" | custom-call | flops 1711276032 | bytes 4194304 | tf_op jit(solution)/shard_map/block_inner/pallas_call | solution.py:343
  40.5 0.5 %collective-permute-start.10 = (f32[8,128]{1,0:T(8,128)S(1)}, f32[8,128]{1,0:T(8,128)S(1)}, u32[]{:S(2)}, u32[]{:S(2)}) collective-permute-start(f32[8,128]{1,0:T(8,128)S(1)} %get-tuple-element.54), channel_id=1, source_target_pairs={{0,1},{1,0},{2,3},{3,2},{4,5},{5,4},{6,7},{7,6},{8,9},{9,8},{10,11... | collective-permute-start | bytes 12296 | tf_op jit(solution)/shard_map/ppermute | solution.py:369
  41.0 0.0 collective-permute-done.11.refs_5_
  41.0 2.5 %collective-permute-done.12.refs_6_ = f32[4,128,128]{2,1,0:T(8,128)S(1)} collective-permute-done((f32[4,128,128]{2,1,0:T(8,128)S(1)}, f32[4,128,128]{2,1,0:T(8,128)S(1)}, u32[]{:S(2)}, u32[]{:S(2)}) %collective-permute-start.12) | collective-permute-done | bytes 262176 | tf_op jit(solution)/shard_map/ppermute | solution.py:454
  43.5 1.0 %collective-permute-start.13 = (f32[8,128]{1,0:T(8,128)S(1)}, f32[8,128]{1,0:T(8,128)S(1)}, u32[]{:S(2)}, u32[]{:S(2)}) collective-permute-start(f32[8,128]{1,0:T(8,128)S(1)} %pad_maximum_fusion.1), channel_id=1, source_target_pairs={{0,1},{1,0},{2,3},{3,2},{4,5},{5,4},{6,7},{7,6},{8,9},{9,8},{10,11... | collective-permute-start | bytes 12296 | tf_op jit(solution)/shard_map/ppermute | solution.py:369
  44.6 0.0 collective-permute-done.9.refs_3_
  44.6 0.0 collective-permute-done.10.refs_4_
  44.6 2.3 %block_inner.3.refs_12_ = f32[4,2048,128]{2,1,0:T(8,128)S(1)} custom-call(f32[4,2,512,128]{3,2,1,0:T(8,128)S(1)} %get-tuple-element.57.refs_0_, f32[4,2,128,128]{3,2,1,0:T(8,128)S(1)} %get-tuple-element.51.refs_1_, f32[4,2,128,128]{3,2,1,0:T(8,128)S(1)} %get-tuple-element.52.refs_2_, f32[8,128]{1,0:T(8,128)S(1)} %collective-permute-done.9.refs_3_, ...), custom_call_target="tpu_custom_call" | custom-call | flops 1308622848 | bytes 4194304 | tf_op jit(solution)/shard_map/block_inner/pallas_call | solution.py:343
  46.9 0.0 collective-permute-done.13.refs_7_
  47.0 4.2 %block_border.3 = (f32[4,2048,128]{2,1,0:T(8,128)}, f32[4,2048,128]{2,1,0:T(8,128)S(1)}) custom-call(f32[4,2,512,128]{3,2,1,0:T(8,128)S(1)} %get-tuple-element.50.refs_11_.refs_0_, f32[4,2,128,128]{3,2,1,0:T(8,128)S(1)} %get-tuple-element.51.refs_1_, f32[4,2,128,128]{3,2,1,0:T(8,128)S(1)} %get-tuple-element.52.refs_2_, ...), custom_call_target="tpu_custom_call", output_to_operand_aliasing={{1}: (12, {})} | custom-call | flops 1308622848 | bytes 4194304 | tf_op jit(solution)/shard_map/block_border/pallas_call | solution.py:343
  (5 shorter events, 0.1 us)
Async XLA Ops:
  1.0 9.5 %collective-permute-start = (f32[72,512]{1,0:T(8,128)S(1)}, f32[72,512]{1,0:T(8,128)S(1)}, u32[]{:S(2)}, u32[]{:S(2)}) collective-permute-start(f32[72,512]{1,0:T(8,128)S(1)} %pack_first.1.first.refs_14_.refs_9_), channel_id=1, source_target_pairs={{0,2},{1,3},{4,6},{5,7},{8,10},{9,11},{12,14},{13,15},{16,18},{17,... | collective-permute-start | bytes 442376 | tf_op jit(solution)/shard_map/ppermute | solution.py:374
  5.3 11.9 %collective-permute-start.7 = (f32[832,128]{1,0:T(8,128)S(1)}, f32[832,128]{1,0:T(8,128)S(1)}, u32[]{:S(2)}, u32[]{:S(2)}) collective-permute-start(f32[832,128]{1,0:T(8,128)S(1)} %pack_rest.1), channel_id=1, source_target_pairs={{0,2},{1,3},{4,6},{5,7},{8,10},{9,11},{12,14},{13,15},{16,18},{17,... | collective-permute-start | bytes 1277960 | tf_op jit(solution)/shard_map/ppermute | solution.py:374
  10.4 2.0 %collective-permute-start.1 = (f32[72,512]{1,0:T(8,128)S(1)}, f32[72,512]{1,0:T(8,128)S(1)}, u32[]{:S(2)}, u32[]{:S(2)}) collective-permute-start(f32[72,512]{1,0:T(8,128)S(1)} %collective-permute-done.mine), channel_id=1, source_target_pairs={{0,1},{1,0},{2,3},{3,2},{4,5},{5,4},{6,7},{7,6},{8,9},{9,8},{10,11... | collective-permute-start | bytes 442376 | tf_op jit(solution)/shard_map/ppermute | solution.py:369
  14.0 7.8 %collective-permute-start.4 = (f32[4,128,128]{2,1,0:T(8,128)}, f32[4,128,128]{2,1,0:T(8,128)}, u32[]{:S(2)}, u32[]{:S(2)}) collective-permute-start(f32[4,128,128]{2,1,0:T(8,128)} %get-tuple-element.42), channel_id=1, source_target_pairs={{0,4},{4,0},{8,12},{12,8},{1,5},{5,1},{9,13},{13,9},{2,6},{6,2},{1... | collective-permute-start | bytes 786440 | tf_op jit(solution)/shard_map/ppermute | solution.py:453
  15.3 9.4 %collective-permute-start.5 = (f32[4,128,128]{2,1,0:T(8,128)}, f32[4,128,128]{2,1,0:T(8,128)}, u32[]{:S(2)}, u32[]{:S(2)}) collective-permute-start(f32[4,128,128]{2,1,0:T(8,128)} %get-tuple-element.43), channel_id=1, source_target_pairs={{4,8},{8,4},{5,9},{9,5},{6,10},{10,6},{7,11},{11,7},{20,24},{24,20... | collective-permute-start | bytes 786440 | tf_op jit(solution)/shard_map/ppermute | solution.py:454
  17.2 9.8 %collective-permute-start.8 = (f32[832,128]{1,0:T(8,128)S(1)}, f32[832,128]{1,0:T(8,128)S(1)}, u32[]{:S(2)}, u32[]{:S(2)}) collective-permute-start(f32[832,128]{1,0:T(8,128)S(1)} %collective-permute-done.7.mine), channel_id=1, source_target_pairs={{0,1},{1,0},{2,3},{3,2},{4,5},{5,4},{6,7},{7,6},{8,9},{9,8},{10,11... | collective-permute-start | bytes 1277960 | tf_op jit(solution)/shard_map/ppermute | solution.py:369
  17.9 9.2 %collective-permute-start.2 = (f32[8,128]{1,0:T(8,128)S(1)}, f32[8,128]{1,0:T(8,128)S(1)}, u32[]{:S(2)}, u32[]{:S(2)}) collective-permute-start(f32[8,128]{1,0:T(8,128)S(1)} %get-tuple-element.40), channel_id=1, source_target_pairs={{0,1},{1,0},{2,3},{3,2},{4,5},{5,4},{6,7},{7,6},{8,9},{9,8},{10,11... | collective-permute-start | bytes 12296 | tf_op jit(solution)/shard_map/ppermute | solution.py:369
  21.0 6.1 %collective-permute-start.3 = (f32[8,128]{1,0:T(8,128)S(1)}, f32[8,128]{1,0:T(8,128)S(1)}, u32[]{:S(2)}, u32[]{:S(2)}) collective-permute-start(f32[8,128]{1,0:T(8,128)S(1)} %get-tuple-element.41), channel_id=1, source_target_pairs={{0,1},{1,0},{2,3},{3,2},{4,5},{5,4},{6,7},{7,6},{8,9},{9,8},{10,11... | collective-permute-start | bytes 12296 | tf_op jit(solution)/shard_map/ppermute | solution.py:369
  25.4 2.4 %collective-permute-start.6 = (f32[8,128]{1,0:T(8,128)S(1)}, f32[8,128]{1,0:T(8,128)S(1)}, u32[]{:S(2)}, u32[]{:S(2)}) collective-permute-start(f32[8,128]{1,0:T(8,128)S(1)} %pad_maximum_fusion), channel_id=1, source_target_pairs={{0,1},{1,0},{2,3},{3,2},{4,5},{5,4},{6,7},{7,6},{8,9},{9,8},{10,11... | collective-permute-start | bytes 12296 | tf_op jit(solution)/shard_map/ppermute | solution.py:369
  33.4 7.6 %collective-permute-start.11 = (f32[4,128,128]{2,1,0:T(8,128)S(1)}, f32[4,128,128]{2,1,0:T(8,128)S(1)}, u32[]{:S(2)}, u32[]{:S(2)}) collective-permute-start(f32[4,128,128]{2,1,0:T(8,128)S(1)} %get-tuple-element.55), channel_id=1, source_target_pairs={{0,4},{4,0},{8,12},{12,8},{1,5},{5,1},{9,13},{13,9},{2,6},{6,2},{1... | collective-permute-start | bytes 786440 | tf_op jit(solution)/shard_map/ppermute | solution.py:453
  33.5 11.1 %collective-permute-start.9 = (f32[8,128]{1,0:T(8,128)S(1)}, f32[8,128]{1,0:T(8,128)S(1)}, u32[]{:S(2)}, u32[]{:S(2)}) collective-permute-start(f32[8,128]{1,0:T(8,128)S(1)} %get-tuple-element.53), channel_id=1, source_target_pairs={{0,1},{1,0},{2,3},{3,2},{4,5},{5,4},{6,7},{7,6},{8,9},{9,8},{10,11... | collective-permute-start | bytes 12296 | tf_op jit(solution)/shard_map/ppermute | solution.py:369
  33.9 9.6 %collective-permute-start.12 = (f32[4,128,128]{2,1,0:T(8,128)S(1)}, f32[4,128,128]{2,1,0:T(8,128)S(1)}, u32[]{:S(2)}, u32[]{:S(2)}) collective-permute-start(f32[4,128,128]{2,1,0:T(8,128)S(1)} %get-tuple-element.56), channel_id=1, source_target_pairs={{4,8},{8,4},{5,9},{9,5},{6,10},{10,6},{7,11},{11,7},{20,24},{24,20... | collective-permute-start | bytes 786440 | tf_op jit(solution)/shard_map/ppermute | solution.py:454
  40.5 4.1 %collective-permute-start.10 = (f32[8,128]{1,0:T(8,128)S(1)}, f32[8,128]{1,0:T(8,128)S(1)}, u32[]{:S(2)}, u32[]{:S(2)}) collective-permute-start(f32[8,128]{1,0:T(8,128)S(1)} %get-tuple-element.54), channel_id=1, source_target_pairs={{0,1},{1,0},{2,3},{3,2},{4,5},{5,4},{6,7},{7,6},{8,9},{9,8},{10,11... | collective-permute-start | bytes 12296 | tf_op jit(solution)/shard_map/ppermute | solution.py:369
  43.5 3.4 %collective-permute-start.13 = (f32[8,128]{1,0:T(8,128)S(1)}, f32[8,128]{1,0:T(8,128)S(1)}, u32[]{:S(2)}, u32[]{:S(2)}) collective-permute-start(f32[8,128]{1,0:T(8,128)S(1)} %pad_maximum_fusion.1), channel_id=1, source_target_pairs={{0,1},{1,0},{2,3},{3,2},{4,5},{5,4},{6,7},{7,6},{8,9},{9,8},{10,11... | collective-permute-start | bytes 12296 | tf_op jit(solution)/shard_map/ppermute | solution.py:369
where the time goes:
time: 51.6 us; the launch traced here: 51.3 us
  Pallas kernels  27 us (52%)
  starting transfers between devices  15.6 us (30%)
  waiting for transfers between devices  6.77 us (13%)
  local copies, waits for them, and re-layouts  1.46 us (3%)
    pallas_call x12, Pallas kernels, call(): pl.pallas_call(kernel, name=name, in_specs=[spec for _, spec in args], ou...  27 us
    ppermute x8, starting transfers between devices, swap(): return lax.ppermute(array, 'col', [(0, 1), (1, 0)])  5.83 us
    ppermute x2, waiting for transfers between devices, halos(): halo_b = lax.ppermute(msg_b, 'strip', pairs(1))  4.65 us
    ppermute x2, starting transfers between devices, from_section(): lax.ppermute(array, 'section', [(i, i + step) for i in range(sections - s...  4.44 us
    ppermute x2, starting transfers between devices, halos(): halo_b = lax.ppermute(msg_b, 'strip', pairs(1))  4 us
    ppermute x8, waiting for transfers between devices, swap(): return lax.ppermute(array, 'col', [(0, 1), (1, 0)])  1.72 us
    ppermute x2, starting transfers between devices, halos(): halo_a = lax.ppermute(msg_a, 'strip', pairs(0))  1.37 us
  transfers between devices with their start and end apart: 14, of which 5 were waited for; matrix products, arithmetic and copies ran while one was open for 3% of the time, Pallas kernels for 32%

commit v1 on v0

--- a/solution.py
+++ b/solution.py
@@ -48,9 +48,9 @@
 ):
     half = w_reduce.shape[1] // 2
     cm = gain_mid.shape[2]
-    start = pl.multiple_of(lax.axis_index("col") * half, half)
+    low = pl.multiple_of(lax.axis_index("col") * half, half)
     moves = [
-        (w_reduce.at[0, pl.ds(start, half), :], first.at[:half, :]),
+        (w_reduce.at[0, pl.ds(low, half), :], first.at[:half, :]),
         (gain_mid.at[0], gain_held),
         (bias_mid.at[0], bias_held),
         (gain_out, gain_row),
@@ -69,32 +69,38 @@
     first[half + 2 : half + 3, :] = bias_row[...]
 
 
-def pack_rest_kernel(w_spatial, w_expand, rest, sem):
+def pack_rest_kernel(w_spatial, w_expand, before, rest, sem):
     half = w_spatial.shape[2] // 2
     wide = w_expand.shape[1] // 2
     low = pl.multiple_of(lax.axis_index("col") * half, half)
     at = pl.multiple_of(lax.axis_index("col") * wide, wide)
-    copies = [
-        pltpu.make_async_copy(
-            w_spatial.at[0, tap, pl.ds(low, half), :], rest.at[tap * half : (tap + 1) * half, :], sem.at[tap]
-        )
-        for tap in range(9)
-    ]
-    copies.append(
-        pltpu.make_async_copy(w_expand.at[0, pl.ds(at, wide), :], rest.at[9 * half :, :], sem.at[9])
-    )
+    moves = [(w_expand.at[0, pl.ds(at, wide), :], rest.at[9 * half :, :])]
+    for tap in range(9):
+        moves.append((w_spatial.at[0, tap, pl.ds(low, half), :], rest.at[tap * half : (tap + 1) * half, :]))
+    copies = [pltpu.make_async_copy(here, there, sem.at[i]) for i, (here, there) in enumerate(moves)]
     for copy in copies:
         copy.start()
     for copy in copies:
         copy.wait()
 
 
-def fetch_kernel(x, held, sem):
-    copies = [pltpu.make_async_copy(x.at[t], held.at[t], sem.at[t]) for t in range(x.shape[0])]
+def fetch_kernel(x, w_reduce, before, x_held, w_held, sem):
+    copies = [pltpu.make_async_copy(x.at[t], x_held.at[t], sem.at[t]) for t in range(x.shape[0])]
+    copies.append(pltpu.make_async_copy(w_reduce.at[0], w_held, sem.at[x.shape[0]]))
     for copy in copies:
         copy.start()
     for copy in copies:
         copy.wait()
+
+
+def corner_kernel(halo_a, halo_b, *refs):
+    out = refs[-1]
+    first = first_core()
+    tiles, cols = halo_a.shape[:2]
+    for i, halo in enumerate((halo_a, halo_b)):
+        for tile in range(tiles):
+            side = jnp.where(first, halo[tile, cols - 1 : cols, :], halo[tile, 0:1, :])
+            out[i * tiles + tile : i * tiles + tile + 1, :] = side
 
 
 def store_reduce(w_high, at, rows):
@@ -116,22 +122,22 @@
     w_expand[:, 2 * cm :] = high
 
 
-def prepare_own_kernel(w_reduce, w_spatial, w_expand, first, out_reduce, out_spatial, out_expand, out_shift, out_terms):
-    half = w_reduce.shape[1] // 2
-    store_reduce(out_reduce, 0, w_reduce[0])
+def prepare_own_kernel(w_reduce, w_spatial, w_expand, first, before, out_reduce, out_spatial, out_expand, out_shift, out_terms):
+    half = w_reduce.shape[0] // 2
+    store_reduce(out_reduce, 0, w_reduce[...])
     terms = first[half : half + 8, :]
     out_terms[...] = terms
     out_shift[...] = column_of(terms[2:3, :])
     store_rest(lambda tap: w_spatial[0, tap], w_expand[0], terms[1:2, :], out_spatial, out_expand)
 
 
-def prepare_reduce_kernel(level, mine, other, own_reduce, own_terms, out_reduce, out_terms):
+def prepare_reduce_kernel(level, mine, other, w_reduce, first, out_reduce, out_terms):
     half = mine.shape[0] - 8
 
     @pl.when(lax.axis_index("section") == level)
     def _():
-        out_reduce[...] = own_reduce[...]
-        out_terms[...] = own_terms[...]
+        store_reduce(out_reduce, 0, w_reduce[...])
+        out_terms[...] = first[half:, :]
 
     @pl.when(lax.axis_index("section") != level)
     def _():
@@ -203,25 +209,10 @@
     return x[tile, j]
 
 
-def bring(x, held, sem, start):
-    copies = [pltpu.make_async_copy(x.at[t], held.at[t], sem.at[t]) for t in range(x.shape[0])]
-    if start:
-        for copy in copies:
-            copy.start()
-    return copies
-
-
-def reduce_kernel(kind, rows, x, w_reduce, terms, r_out, edge, *refs):
-    msgs, copies = refs, None
-    if kind == "inner":
-        msgs = ()
-        copies = bring(x, *refs, True)
-        x = refs[0]
+def reduce_kernel(kind, rows, x, w_reduce, terms, before, r_out, edge, *msgs):
     edge[...] = jnp.zeros_like(edge)
     count = r_out.shape[1]
     for tile in range(x.shape[0]):
-        if copies:
-            copies[tile].wait()
         field = jnp.concatenate([field_rows(x, kind, rows, tile, j) for j in range(count)], axis=1)
         reduce_step(tile, field, w_reduce, terms, r_out, edge, msgs)
 
@@ -250,11 +241,6 @@
         msgs = take(2) if border else []
         edge_out[...] = jnp.zeros_like(edge_out)
     padded, taps_high, taps_low = take(3)
-    copies = None
-    if len(x.shape) == 3:
-        x_held, x_sem = take(2)
-        copies = bring(x, x_held, x_sem, True)
-        x = x_held
     tiles, _, cols, cm = r_border.shape
     chosen = members(kind, rows)
     count = len(chosen)
@@ -276,51 +262,48 @@
         return r_inner[tile, j], edge_inner[at : at + 1, :]
 
     span = count * cols
-    for tile in range(tiles):
-        for i in sorted({r + p for r in chosen for p in (-1, 0, 1)}):
-            field, side = row_and_side(tile, i)
-            slot = padded.at[tile, i + 1]
-            slot[PAD : PAD + cols, :] = field
-            slot[PAD - 1 : PAD, :] = jnp.where(first, 0.0, side)
-            slot[PAD + cols : PAD + cols + 1, :] = jnp.where(first, side, 0.0)
-            for q in range(3):
-                high, low = split(field if q == 1 else slot[PAD - 1 + q : PAD - 1 + q + cols, :])
-                for j, r in enumerate(chosen):
-                    p = i - r + 1
-                    if 0 <= p <= 2:
-                        lanes = slice((3 * p + q) * cm, (3 * p + q + 1) * cm)
-                        at = (tile * count + j) * cols
-                        taps_high[at : at + cols, lanes] = high
-                        taps_low[at : at + cols, lanes] = low
-    group = 4
-    middles = []
+    group = 2 if last and border and tiles % 2 == 0 else tiles
     for g in range(0, tiles, group):
+        for tile in range(g, g + group):
+            for i in sorted({r + p for r in chosen for p in (-1, 0, 1)}):
+                field, side = row_and_side(tile, i)
+                slot = padded.at[tile, i + 1]
+                slot[PAD : PAD + cols, :] = field
+                slot[PAD - 1 : PAD, :] = jnp.where(first, 0.0, side)
+                slot[PAD + cols : PAD + cols + 1, :] = jnp.where(first, side, 0.0)
+                for q in range(3):
+                    high, low = split(field if q == 1 else slot[PAD - 1 + q : PAD - 1 + q + cols, :])
+                    for j, r in enumerate(chosen):
+                        p = i - r + 1
+                        if 0 <= p <= 2:
+                            lanes = slice((3 * p + q) * cm, (3 * p + q + 1) * cm)
+                            at = (tile * count + j) * cols
+                            taps_high[at : at + cols, lanes] = high
+                            taps_low[at : at + cols, lanes] = low
         at = slice(g * span, (g + group) * span)
         both = dot(taps_high[at, :], w_spatial[...])
         spatial = both[:, :cm] + both[:, cm:] + dot(taps_low[at, :], w_spatial[:, :cm])
         high, low = split(jnp.maximum(spatial * gain + shift, 0.0))
-        middles.append(jnp.concatenate([high, high, low], axis=1))
-    for tile in range(tiles):
-        g, k = tile // group, tile % group
-        branch = dot_nt(w_expand[...], middles[g][k * span : (k + 1) * span])
-        after = []
-        if copies:
-            copies[tile].wait()
-        for j in range(count):
-            before = field_rows(x, kind, rows, tile, j)
-            new = jnp.maximum(before + branch[:, j * cols : (j + 1) * cols] + shift_out[...], 0.0)
-            after.append(jnp.where(keep, new, before))
-            if last:
-                whole = outs[-1]
-                whole[tile, pl.ds(chosen[j], whole.shape[1] // rows, stride=rows), :] = after[j]
-            else:
-                outs[0][tile, j] = after[j]
-        if not last:
-            field = jnp.concatenate(after, axis=1)
-            reduce_step(tile, field, next_reduce, next_terms, r_out, edge_out, msgs)
-        if last and border:
-            sem = refs[0]
-            pltpu.make_async_copy(outs[1].at[tile], outs[0].at[tile], sem.at[tile]).start()
+        middle = jnp.concatenate([high, high, low], axis=1)
+        for tile in range(g, g + group):
+            k = tile - g
+            branch = dot_nt(w_expand[...], middle[k * span : (k + 1) * span])
+            after = []
+            for j in range(count):
+                before = field_rows(x, kind, rows, tile, j)
+                new = jnp.maximum(before + branch[:, j * cols : (j + 1) * cols] + shift_out[...], 0.0)
+                after.append(jnp.where(keep, new, before))
+                if last:
+                    whole = outs[-1]
+                    whole[tile, pl.ds(chosen[j], whole.shape[1] // rows, stride=rows), :] = after[j]
+                else:
+                    outs[0][tile, j] = after[j]
+            if not last:
+                field = jnp.concatenate(after, axis=1)
+                reduce_step(tile, field, next_reduce, next_terms, r_out, edge_out, msgs)
+            if last and border:
+                sem = refs[0]
+                pltpu.make_async_copy(outs[1].at[tile], outs[0].at[tile], sem.at[tile]).start()
     if last and border:
         sem = refs[0]
         for tile in range(tiles):
@@ -348,7 +331,7 @@
         out_shape=outs,
         scratch_shapes=list(scratch),
         input_output_aliases=aliases or {},
-        compiler_params=pltpu.CompilerParams(vmem_limit_bytes=24 * 2**20),
+        compiler_params=pltpu.CompilerParams(vmem_limit_bytes=16 * 2**20),
         cost_estimate=pl.CostEstimate(flops=flops, bytes_accessed=moved, transcendentals=0),
     )(*arrays)
 
@@ -357,8 +340,6 @@
     sections = lax.axis_size("section")
     strips = lax.axis_size("strip")
     section = lax.axis_index("section")
-    strip = lax.axis_index("strip")
-    core = lax.axis_index("col")
     tiles, c, rows, cols = x_in.shape
     cm = w_reduce.shape[1]
     half, wide = cm // 2, c // 2
@@ -375,55 +356,60 @@
             total = sent if total is None else jnp.where(section - level == step, sent, total)
         return total
 
-    def pairs(start):
+    def pairs(start, level):
         found = []
         for i in range(start, strips - 1, 2):
-            found += [(i, i + 1), (i + 1, i)]
+            for j in range(level, sections):
+                above, below = i * sections + j, (i + 1) * sections + j
+                found += [(above, below), (below, above)]
         return found
 
     (first,) = call(
-        pack_first_kernel, "pack_first",
-        [(a, HBM) for a in (w_reduce, gain_mid, bias_mid, gain_out, bias_out)],
+        pack_first_kernel, "pack_first", [(a, HBM) for a in (w_reduce, gain_mid, bias_mid, gain_out, bias_out)],
         [near((half + 8, c))],
         [pltpu.VMEM((2, cm), F32)] * 2 + [pltpu.VMEM((1, c), F32)] * 2 + [pltpu.SemaphoreType.DMA((5,))],
         moved=4 * half * c,
     )
     first_sent = [from_section(first, level) for level in range(sections - 1)]
+    flat = x_in.reshape(tiles, c * rows, cols)
+    held, w_held = call(
+        fetch_kernel, "fetch", [(flat, HBM), (w_reduce, HBM), (first, ANY)], [near(flat.shape), near((cm, c))],
+        [pltpu.SemaphoreType.DMA((tiles + 1,))], moved=4 * cells * c,
+    )
     (rest,) = call(
-        pack_rest_kernel, "pack_rest", [(w_spatial, HBM), (w_expand, HBM)],
+        pack_rest_kernel, "pack_rest", [(w_spatial, HBM), (w_expand, HBM), (w_held, ANY)],
         [near((9 * half + wide, cm))], [pltpu.SemaphoreType.DMA((10,))], moved=4 * (9 * half + wide) * cm,
     )
     rest_sent = [from_section(rest, level) for level in range(sections - 1)]
-    flat = x_in.reshape(tiles, c * rows, cols)
-    (held,) = call(
-        fetch_kernel, "fetch", [(flat, HBM)], [near(flat.shape)], [pltpu.SemaphoreType.DMA((tiles,))],
-        moved=4 * cells * c,
-    )
     rest_shapes = [near((9 * cm, 2 * cm), BF16), near((c, 3 * cm), BF16), near((c, 128))]
-    own_reduce, own_spatial, own_expand, own_shift, own_terms = call(
-        prepare_own_kernel, "prepare_own", [(w_reduce, FAR), (w_spatial, FAR), (w_expand, FAR), (first, VMEM)],
-        [near((2 * cm, c), BF16)] + rest_shapes + [near((8, c))], moved=4 * cm * (2 * c + 9 * cm),
-    )
-
-    first_sent, held, _ = lax.optimization_barrier((first_sent, held, own_reduce))
+    first_sent, held, w_held, _ = lax.optimization_barrier((first_sent, held, w_held, rest))
+
+    def prepare_own(before):
+        return call(
+            prepare_own_kernel, "prepare_own",
+            [(w_held, VMEM), (w_spatial, FAR), (w_expand, FAR), (first, VMEM), (before, ANY)],
+            [near((2 * cm, c), BF16)] + rest_shapes + [near((8, c))], moved=4 * cm * (2 * c + 9 * cm),
+        )
 
     def reduce_weights(level):
-        if level == sections - 1:
-            return own_reduce, own_terms
+        if level == sections - 1 and level > 0:
+            return own[0], own[4]
+        if sections == 1:
+            return prepare_own(first)[::4]
         mine = first_sent[level]
         return call(
             functools.partial(prepare_reduce_kernel, level), "prepare_reduce",
-            [(a, VMEM) for a in (mine, swap(mine), own_reduce, own_terms)],
+            [(a, VMEM) for a in (mine, swap(mine), w_held, first)],
             [near((2 * cm, c), BF16), near((8, c))], moved=4 * cm * c,
         )
 
     def rest_weights(level, terms):
         if level == sections - 1:
-            return own_spatial, own_expand, own_shift
-        mine = rest_sent[level]
+            return own[1:4]
+        mine, _ = lax.optimization_barrier((rest_sent[level], halo[3]))
         return call(
             functools.partial(prepare_rest_kernel, level), "prepare_rest",
-            [(a, VMEM) for a in (mine, swap(mine), terms, own_spatial, own_expand, own_shift)],
+            [(a, VMEM) for a in (mine, swap(mine), terms, *own[1:4])],
             rest_shapes, moved=4 * cm * (c + 9 * cm),
         )
 
@@ -432,14 +418,12 @@
         shapes = [near((tiles, count, cols, cm)), near((-(-tiles * count // 8) * 8, cm))]
         return shapes + ([near((tiles, cols, cm))] * 2 if kind == "border" else [])
 
-    def reduce_call(kind, level, weights):
+    def reduce_call(kind, level, weights, before):
         return call(
             functools.partial(reduce_kernel, kind, rows), "reduce_" + kind,
-            [(held, VMEM) if kind == "border" else (flat, HBM)] + [(a, VMEM) for a in weights],
-            reduced_shapes(kind), [] if kind == "border" else tile_scratch, flops=3 * cells * c * cm, moved=4 * cells * c // 2,
+            [(held, VMEM)] + [(a, VMEM) for a in weights] + [(before, ANY)],
+            reduced_shapes(kind), flops=3 * cells * c * cm, moved=4 * cells * c // 2,
         )
-
-    tile_scratch = [pltpu.VMEM(flat.shape, F32), pltpu.SemaphoreType.DMA((tiles,))]
 
     def scratch(kind):
         count = 2 if kind == "border" else inner
@@ -449,29 +433,29 @@
             pltpu.VMEM((tiles * count * cols, 9 * cm), BF16),
         ]
 
-    def halos(msg_a, msg_b):
-        halo_a = lax.ppermute(msg_a, "strip", pairs(0))
-        halo_b = lax.ppermute(msg_b, "strip", pairs(1))
-        at = jnp.where(core == 0, cols - 1, 0)
-        edge_a = lax.dynamic_slice_in_dim(halo_a, at, 1, 1)
-        edge_b = lax.dynamic_slice_in_dim(halo_b, at, 1, 1)
-        return halo_a, halo_b, swap(jnp.concatenate([edge_a[:, 0], edge_b[:, 0]], axis=0))
+    def halos(msg_a, msg_b, swapped, level):
+        axes = ("strip", "section")
+        msg_a, _ = lax.optimization_barrier((msg_a, swapped))
+        return lax.ppermute(msg_a, axes, pairs(0, level)), lax.ppermute(msg_b, axes, pairs(1, level))
+
+    def with_corners(halo, before):
+        args = [(a, VMEM) for a in halo] + [(a, ANY) for a in before]
+        (corners,) = call(corner_kernel, "corners", args, [near((2 * tiles, cm))])
+        return halo + (swap(corners), corners)
 
     def block_call(kind, level, x, sent, weights, next_weights, before, halo=None):
         last = level == sections - 1
         (r_border, edge_border), (r_inner, edge_inner) = sent
-        args = [(x, HBM if x is flat else VMEM)]
+        args = [(x, VMEM)]
         args += [(a, VMEM) for a in (r_border, r_inner, edge_border, edge_inner)]
         if kind == "border":
-            args += [(a, VMEM) for a in halo]
+            args += [(a, VMEM) for a in halo[:3]]
         args += [(a, VMEM) for a in weights]
         if not last:
             args += [(a, VMEM) for a in next_weights]
         args.append((before, VMEM if last and kind == "border" else ANY))
         count = 2 if kind == "border" else inner
         more, out_specs, aliases, held_out = scratch(kind), None, None, near((tiles, count, c, cols))
-        if x is flat:
-            more += tile_scratch
         if last:
             held_out = near(flat.shape)
         outs = [held_out] + ([] if last else reduced_shapes(kind))
@@ -486,23 +470,33 @@
         )
 
     weights = reduce_weights(0)
-    border = reduce_call("border", 0, weights)
-    halo = halos(border[2], border[3])
-    inside = reduce_call("inner", 0, weights)
-    x_border = x_inner = flat
+    border = reduce_call("border", 0, weights, first)
+    edges = swap(border[1])
+    halo = halos(border[2], border[3], edges, 0)
+    own = prepare_own(border[1])
+    inside = reduce_call("inner", 0, weights, border[1])
+    sent = ((border[0], edges), (inside[0], swap(inside[1])))
+    halo = with_corners(halo, (own[4], sent[0][1], sent[1][1]))
+    x_border = x_inner = held
     for level in range(sections):
         last = level == sections - 1
         terms = weights[1]
         rest_of = tuple(rest_weights(level, terms)) + (terms,)
-        sent = ((border[0], swap(border[1])), (inside[0], swap(inside[1])))
+        if level > 0:
+            sent = ((border[0], edges), (inside[0], swap(inside[1])))
         if last:
             (part,) = block_call("inner", level, x_inner, sent, rest_of, None, first)
+            if level > 0:
+                halo = with_corners(halo, (part,))
             whole = block_call("border", level, x_border, sent, rest_of, None, part, halo)[0]
         else:
             weights = reduce_weights(level + 1)
             x_border, *border = block_call("border", level, x_border, sent, rest_of, weights, first, halo)
-            halo = halos(border[2], border[3])
+            edges = swap(border[1])
+            halo = halos(border[2], border[3], edges, level + 1)
             x_inner, *inside = block_call("inner", level, x_inner, sent, rest_of, weights, x_border)
+            if level + 1 < sections - 1:
+                halo = with_corners(halo, (inside[1],))
     return whole.reshape(1, tiles, c, rows, cols)
 
 

time: 51.6 us -> 48.5 us (0.940)
  the two profiles are of different devices: /device:TPU:17 before, /device:TPU:15 now
where the time goes in v1:
time: 48.5 us; the launch traced here: 47.7 us
  Pallas kernels  20.8 us (43%)
  starting transfers between devices  16.8 us (35%)
  waiting for transfers between devices  9.83 us (20%)
    pallas_call x14, Pallas kernels, call(): pl.pallas_call(kernel, name=name, in_specs=[spec for _, spec in args], ou...  20.8 us
    ppermute x2, starting transfers between devices, halos(): lax.ppermute(msg_b, axes, pairs(1, level))  6.2 us
    ppermute x8, starting transfers between devices, swap(): return lax.ppermute(array, 'col', [(0, 1), (1, 0)])  5.82 us
    ppermute x8, waiting for transfers between devices, swap(): return lax.ppermute(array, 'col', [(0, 1), (1, 0)])  2.98 us
    ppermute x2, waiting for transfers between devices, halos(): lax.ppermute(msg_b, axes, pairs(1, level))  2.93 us
    ppermute x2, waiting for transfers between devices, from_section(): lax.ppermute(array, 'section', [(i, i + step) for i in range(sections - s...  2.72 us
    ppermute x2, starting transfers between devices, from_section(): lax.ppermute(array, 'section', [(i, i + step) for i in range(sections - s...  2.57 us
    ppermute x2, starting transfers between devices, halos(): lax.ppermute(msg_a, axes, pairs(0, level))  2.17 us
  transfers between devices with their start and end apart: 14, of which 8 were waited for; matrix products, arithmetic and copies ran while one was open for 0% of the time, Pallas kernels for 26%

profile of v1, /device:TPU:15, one launch (start us, length us, event | category | flops | bytes accessed | tf_op | source)
XLA Modules:
  0.0 47.7 jit_solution(10289840210627900953)
XLA Ops:
  0.0 1.0 %pack_first.1.before.first.refs_14_.refs_9_ = f32[72,512]{1,0:T(8,128)S(1)} custom-call(f32[1,128,512]{2,1,0:T(8,128)} %w_reduce.3, f32[1,2,128]{2,1,0:T(2,128)} %gain_mid.1, f32[1,2,128]{2,1,0:T(2,128)} %bias_mid.1, f32[1,512]{1,0:T(1,128)} %gain_out.1, f32[1,512]{1,0:T(1,128)} %bias_out.1), custom_call_target="tpu_custom_call" | custom-call | bytes 131072 | tf_op jit(solution)/shard_map/pack_first/pallas_call | solution.py:326
  1.0 1.3 %collective-permute-start = (f32[72,512]{1,0:T(8,128)S(1)}, f32[72,512]{1,0:T(8,128)S(1)}, u32[]{:S(2)}, u32[]{:S(2)}) collective-permute-start(f32[72,512]{1,0:T(8,128)S(1)} %pack_first.1.before.first.refs_14_.refs_9_), channel_id=1, source_target_pairs={{0,2},{1,3},{4,6},{5,7},{8,10},{9,11},{12,14},{13,15},{16,18},{17,... | collective-permute-start | bytes 442376 | tf_op jit(solution)/shard_map/ppermute | solution.py:355
  2.3 2.3 %fetch.1 = (f32[4,2048,128]{2,1,0:T(8,128)S(1)}, f32[128,512]{1,0:T(8,128)S(1)}) custom-call(f32[4,2048,128]{2,1,0:T(8,128)} %bitcast.2, f32[1,128,512]{2,1,0:T(8,128)} %w_reduce.3, f32[72,512]{1,0:T(8,128)S(1)} %pack_first.1.before.first.refs_14_.refs_9_), custom_call_target="tpu_custom_call" | custom-call | bytes 4194304 | tf_op jit(solution)/shard_map/fetch/pallas_call | solution.py:326
  4.5 1.0 %pack_rest.1 = f32[832,128]{1,0:T(8,128)S(1)} custom-call(f32[1,9,128,128]{3,2,1,0:T(8,128)} %w_spatial.3, f32[1,512,128]{2,1,0:T(8,128)} %w_expand.3, f32[128,512]{1,0:T(8,128)S(1)} %get-tuple-element.42.before.w_reduce), custom_call_target="tpu_custom_call" | custom-call | bytes 425984 | tf_op jit(solution)/shard_map/pack_rest/pallas_call | solution.py:326
  5.6 2.0 %collective-permute-done.mine = f32[72,512]{1,0:T(8,128)S(1)} collective-permute-done((f32[72,512]{1,0:T(8,128)S(1)}, f32[72,512]{1,0:T(8,128)S(1)}, u32[]{:S(2)}, u32[]{:S(2)}) %collective-permute-start) | collective-permute-done | bytes 147488 | tf_op jit(solution)/shard_map/ppermute | solution.py:355
  7.6 1.5 %collective-permute-start.1 = (f32[72,512]{1,0:T(8,128)S(1)}, f32[72,512]{1,0:T(8,128)S(1)}, u32[]{:S(2)}, u32[]{:S(2)}) collective-permute-start(f32[72,512]{1,0:T(8,128)S(1)} %collective-permute-done.mine), channel_id=1, source_target_pairs={{0,1},{1,0},{2,3},{3,2},{4,5},{5,4},{6,7},{7,6},{8,9},{9,8},{10,11... | collective-permute-start | bytes 442376 | tf_op jit(solution)/shard_map/ppermute | solution.py:350
  9.1 1.3 %collective-permute-start.7 = (f32[832,128]{1,0:T(8,128)S(1)}, f32[832,128]{1,0:T(8,128)S(1)}, u32[]{:S(2)}, u32[]{:S(2)}) collective-permute-start(f32[832,128]{1,0:T(8,128)S(1)} %pack_rest.1), channel_id=1, source_target_pairs={{0,2},{1,3},{4,6},{5,7},{8,10},{9,11},{12,14},{13,15},{16,18},{17,... | collective-permute-start | bytes 1277960 | tf_op jit(solution)/shard_map/ppermute | solution.py:355
  10.4 0.0 collective-permute-done.1.other
  10.4 0.1 prepare_reduce.1
  10.5 0.7 %reduce_border.1 = (f32[4,2,128,128]{3,2,1,0:T(8,128)S(1)}, f32[8,128]{1,0:T(8,128)S(1)}, f32[4,128,128]{2,1,0:T(8,128)S(1)}, f32[4,128,128]{2,1,0:T(8,128)S(1)}) custom-call(f32[4,2048,128]{2,1,0:T(8,128)S(1)} %get-tuple-element.40.x.refs_0_, bf16[256,512]{1,0:T(8,128)(2,1)S(1)} %get-tuple-element.43.w_reduce, ...), custom_call_target="tpu_custom_call" | custom-call | flops 402653184 | bytes 2097152 | tf_op jit(solution)/shard_map/reduce_border/pallas_call | solution.py:326
  11.2 0.1 collective-permute-start.2
  11.3 3.2 %collective-permute-start.5 = (f32[4,128,128]{2,1,0:T(8,128)S(1)}, f32[4,128,128]{2,1,0:T(8,128)S(1)}, u32[]{:S(2)}, u32[]{:S(2)}) collective-permute-start(f32[4,128,128]{2,1,0:T(8,128)S(1)} %get-tuple-element.51), channel_id=1, source_target_pairs={{4,8},{8,4},{6,10},{10,6},{5,9},{9,5},{7,11},{11,7},{20,24},{24,20... | collective-permute-start | bytes 786440 | tf_op jit(solution)/shard_map/ppermute | solution.py:439
  14.5 0.0 collective-permute-done.2.refs_1_.refs_3_
  14.5 0.1 collective-permute-start.4
  14.6 0.7 %reduce_inner.1 = (f32[4,2,128,128]{3,2,1,0:T(8,128)S(1)}, f32[8,128]{1,0:T(8,128)S(1)}) custom-call(f32[4,2048,128]{2,1,0:T(8,128)S(1)} %get-tuple-element.40.x.refs_0_, bf16[256,512]{1,0:T(8,128)(2,1)S(1)} %get-tuple-element.43.w_reduce, f32[8,512]{1,0:T(8,128)S(1)} %get-tuple-element.44.terms.refs_11_.refs_8_, f32[8,128]{1,0:T(8,128)S(1)} %get-tuple-element.46.before), custom_call_target="tpu_custom_call" | custom-call | flops 402653184 | bytes 2097152 | tf_op jit(solution)/shard_map/reduce_inner/pallas_call | solution.py:326
  15.4 0.8 %collective-permute-start.3 = (f32[8,128]{1,0:T(8,128)S(1)}, f32[8,128]{1,0:T(8,128)S(1)}, u32[]{:S(2)}, u32[]{:S(2)}) collective-permute-start(f32[8,128]{1,0:T(8,128)S(1)} %get-tuple-element.48), channel_id=1, source_target_pairs={{0,1},{1,0},{2,3},{3,2},{4,5},{5,4},{6,7},{7,6},{8,9},{9,8},{10,11... | collective-permute-start | bytes 12296 | tf_op jit(solution)/shard_map/ppermute | solution.py:350
  16.2 1.5 %prepare_own.1 = (bf16[256,512]{1,0:T(8,128)(2,1)S(1)}, bf16[1152,256]{1,0:T(8,128)(2,1)S(1)}, bf16[512,384]{1,0:T(8,128)(2,1)S(1)}, f32[512,128]{1,0:T(8,128)S(1)}, f32[8,512]{1,0:T(8,128)S(1)}) custom-call(f32[128,512]{1,0:T(8,128)S(1)} %get-tuple-element.42.before.w_reduce, f32[1,9,128,128]{3,2,1,0:T(8,128)} %w_spatial.3, f32[1,512,128]{2,1,0:T(8,128)} %w_expand.3, ...), custom_call_target="tpu_custom_call" | custom-call | bytes 1114112 | tf_op jit(solution)/shard_map/prepare_own/pallas_call | solution.py:326
  17.7 0.0 collective-permute-done.3.refs_2_.refs_4_
  17.7 2.9 %collective-permute-done.5.halo_b.refs_6_ = f32[4,128,128]{2,1,0:T(8,128)S(1)} collective-permute-done((f32[4,128,128]{2,1,0:T(8,128)S(1)}, f32[4,128,128]{2,1,0:T(8,128)S(1)}, u32[]{:S(2)}, u32[]{:S(2)}) %collective-permute-start.5) | collective-permute-done | bytes 262176 | tf_op jit(solution)/shard_map/ppermute | solution.py:439
  20.6 1.1 %collective-permute-done.4.halo_a.refs_5_ = f32[4,128,128]{2,1,0:T(8,128)S(1)} collective-permute-done((f32[4,128,128]{2,1,0:T(8,128)S(1)}, f32[4,128,128]{2,1,0:T(8,128)S(1)}, u32[]{:S(2)}, u32[]{:S(2)}) %collective-permute-start.4) | collective-permute-done | bytes 262176 | tf_op jit(solution)/shard_map/ppermute | solution.py:439
  21.7 0.7 %collective-permute-done.7.mine = f32[832,128]{1,0:T(8,128)S(1)} collective-permute-done((f32[832,128]{1,0:T(8,128)S(1)}, f32[832,128]{1,0:T(8,128)S(1)}, u32[]{:S(2)}, u32[]{:S(2)}) %collective-permute-start.7) | collective-permute-done | bytes 426016 | tf_op jit(solution)/shard_map/ppermute | solution.py:355
  22.5 1.0 %collective-permute-start.8 = (f32[832,128]{1,0:T(8,128)S(1)}, f32[832,128]{1,0:T(8,128)S(1)}, u32[]{:S(2)}, u32[]{:S(2)}) collective-permute-start(f32[832,128]{1,0:T(8,128)S(1)} %collective-permute-done.7.mine), channel_id=1, source_target_pairs={{0,1},{1,0},{2,3},{3,2},{4,5},{5,4},{6,7},{7,6},{8,9},{9,8},{10,11... | collective-permute-start | bytes 1277960 | tf_op jit(solution)/shard_map/ppermute | solution.py:350
  23.4 0.1 collective-permute-start.6
  23.5 1.3 %collective-permute-done.8.other = f32[832,128]{1,0:T(8,128)S(1)} collective-permute-done((f32[832,128]{1,0:T(8,128)S(1)}, f32[832,128]{1,0:T(8,128)S(1)}, u32[]{:S(2)}, u32[]{:S(2)}) %collective-permute-start.8) | collective-permute-done | bytes 426016 | tf_op jit(solution)/shard_map/ppermute | solution.py:350
  24.8 0.4 prepare_rest.1
  25.3 0.0 collective-permute-done.6.refs_7_
  25.3 3.4 %block_border.2 = (f32[4,2,512,128]{3,2,1,0:T(8,128)S(1)}, f32[4,2,128,128]{3,2,1,0:T(8,128)S(1)}, f32[8,128]{1,0:T(8,128)S(1)}, f32[4,128,128]{2,1,0:T(8,128)S(1)}, f32[4,128,128]{2,1,0:T(8,128)S(1)}) custom-call(f32[4,2048,128]{2,1,0:T(8,128)S(1)} %get-tuple-element.40.x.refs_0_, f32[4,2,128,128]{3,2,1,0:T(8,128)S(1)} %get-tuple-element.45.refs_1_, ...), custom_call_target="tpu_custom_call" | custom-call | flops 1711276032 | bytes 4194304 | tf_op jit(solution)/shard_map/block_border/pallas_call | solution.py:326
  28.7 0.4 collective-permute-start.9
  29.0 3.0 %collective-permute-start.12 = (f32[4,128,128]{2,1,0:T(8,128)S(1)}, f32[4,128,128]{2,1,0:T(8,128)S(1)}, u32[]{:S(2)}, u32[]{:S(2)}) collective-permute-start(f32[4,128,128]{2,1,0:T(8,128)S(1)} %get-tuple-element.68), channel_id=1, source_target_pairs={{6,10},{10,6},{7,11},{11,7},{22,26},{26,22},{23,27},{27,23}} | collective-permute-start | bytes 786440 | tf_op jit(solution)/shard_map/ppermute | solution.py:439
  32.1 0.0 collective-permute-done.9.refs_3_
  32.1 2.1 %collective-permute-start.11 = (f32[4,128,128]{2,1,0:T(8,128)S(1)}, f32[4,128,128]{2,1,0:T(8,128)S(1)}, u32[]{:S(2)}, u32[]{:S(2)}) collective-permute-start(f32[4,128,128]{2,1,0:T(8,128)S(1)} %get-tuple-element.67), channel_id=1, source_target_pairs={{2,6},{6,2},{10,14},{14,10},{3,7},{7,3},{11,15},{15,11},{18,22},{2... | collective-permute-start | bytes 786440 | tf_op jit(solution)/shard_map/ppermute | solution.py:439
  34.2 3.3 %block_inner.2 = (f32[4,2,512,128]{3,2,1,0:T(8,128)S(1)}, f32[4,2,128,128]{3,2,1,0:T(8,128)S(1)}, f32[8,128]{1,0:T(8,128)S(1)}) custom-call(f32[4,2048,128]{2,1,0:T(8,128)S(1)} %get-tuple-element.40.x.refs_0_, f32[4,2,128,128]{3,2,1,0:T(8,128)S(1)} %get-tuple-element.45.refs_1_, f32[4,2,128,128]{3,2,1,0:T(8,128)S(1)} %get-tuple-element.47.refs_2_, ...), custom_call_target="tpu_custom_call" | custom-call | flops 1711276032 | bytes 4194304 | tf_op jit(solution)/shard_map/block_inner/pallas_call | solution.py:326
  37.5 0.5 %collective-permute-start.10 = (f32[8,128]{1,0:T(8,128)S(1)}, f32[8,128]{1,0:T(8,128)S(1)}, u32[]{:S(2)}, u32[]{:S(2)}) collective-permute-start(f32[8,128]{1,0:T(8,128)S(1)} %get-tuple-element.65), channel_id=1, source_target_pairs={{0,1},{1,0},{2,3},{3,2},{4,5},{5,4},{6,7},{7,6},{8,9},{9,8},{10,11... | collective-permute-start | bytes 12296 | tf_op jit(solution)/shard_map/ppermute | solution.py:350
  38.0 0.8 %collective-permute-done.10.refs_4_ = f32[8,128]{1,0:T(8,128)S(1)} collective-permute-done((f32[8,128]{1,0:T(8,128)S(1)}, f32[8,128]{1,0:T(8,128)S(1)}, u32[]{:S(2)}, u32[]{:S(2)}) %collective-permute-start.10) | collective-permute-done | bytes 4128 | tf_op jit(solution)/shard_map/ppermute | solution.py:350
  38.9 2.4 %block_inner.3.refs_0_.refs_12_ = f32[4,2048,128]{2,1,0:T(8,128)S(1)} custom-call(f32[4,2,512,128]{3,2,1,0:T(8,128)S(1)} %get-tuple-element.69.refs_0_, f32[4,2,128,128]{3,2,1,0:T(8,128)S(1)} %get-tuple-element.62.refs_1_, f32[4,2,128,128]{3,2,1,0:T(8,128)S(1)} %get-tuple-element.63.refs_2_, f32[8,128]{1,0:T(8,128)S(1)} %collective-permute-done.9.refs_3_, ...), custom_call_target="tpu_custom_call" | custom-call | flops 1308622848 | bytes 4194304 | tf_op jit(solution)/shard_map/block_inner/pallas_call | solution.py:326
  41.2 0.0 collective-permute-done.12.halo_b.refs_6_
  41.2 0.1 collective-permute-done.11.halo_a.refs_5_
  41.4 1.4 %collective-permute-start.13 = (f32[8,128]{1,0:T(8,128)S(1)}, f32[8,128]{1,0:T(8,128)S(1)}, u32[]{:S(2)}, u32[]{:S(2)}) collective-permute-start(f32[8,128]{1,0:T(8,128)S(1)} %corners.3), channel_id=1, source_target_pairs={{0,1},{1,0},{2,3},{3,2},{4,5},{5,4},{6,7},{7,6},{8,9},{9,8},{10,11... | collective-permute-start | bytes 12296 | tf_op jit(solution)/shard_map/ppermute | solution.py:350
  42.8 0.8 %collective-permute-done.13.refs_7_ = f32[8,128]{1,0:T(8,128)S(1)} collective-permute-done((f32[8,128]{1,0:T(8,128)S(1)}, f32[8,128]{1,0:T(8,128)S(1)}, u32[]{:S(2)}, u32[]{:S(2)}) %collective-permute-start.13) | collective-permute-done | bytes 4128 | tf_op jit(solution)/shard_map/ppermute | solution.py:350
  43.6 4.0 %block_border.3 = (f32[4,2048,128]{2,1,0:T(8,128)}, f32[4,2048,128]{2,1,0:T(8,128)S(1)}) custom-call(f32[4,2,512,128]{3,2,1,0:T(8,128)S(1)} %get-tuple-element.61.refs_11_.refs_0_, f32[4,2,128,128]{3,2,1,0:T(8,128)S(1)} %get-tuple-element.62.refs_1_, f32[4,2,128,128]{3,2,1,0:T(8,128)S(1)} %get-tuple-element.63.refs_2_, ...), custom_call_target="tpu_custom_call", output_to_operand_aliasing={{1}: (12, {})} | custom-call | flops 1308622848 | bytes 4194304 | tf_op jit(solution)/shard_map/block_border/pallas_call | solution.py:326
  (2 shorter events, 0.0 us)
Async XLA Ops:
  1.0 6.6 %collective-permute-start = (f32[72,512]{1,0:T(8,128)S(1)}, f32[72,512]{1,0:T(8,128)S(1)}, u32[]{:S(2)}, u32[]{:S(2)}) collective-permute-start(f32[72,512]{1,0:T(8,128)S(1)} %pack_first.1.before.first.refs_14_.refs_9_), channel_id=1, source_target_pairs={{0,2},{1,3},{4,6},{5,7},{8,10},{9,11},{12,14},{13,15},{16,18},{17,... | collective-permute-start | bytes 442376 | tf_op jit(solution)/shard_map/ppermute | solution.py:355
  7.6 2.8 %collective-permute-start.1 = (f32[72,512]{1,0:T(8,128)S(1)}, f32[72,512]{1,0:T(8,128)S(1)}, u32[]{:S(2)}, u32[]{:S(2)}) collective-permute-start(f32[72,512]{1,0:T(8,128)S(1)} %collective-permute-done.mine), channel_id=1, source_target_pairs={{0,1},{1,0},{2,3},{3,2},{4,5},{5,4},{6,7},{7,6},{8,9},{9,8},{10,11... | collective-permute-start | bytes 442376 | tf_op jit(solution)/shard_map/ppermute | solution.py:350
  9.1 13.3 %collective-permute-start.7 = (f32[832,128]{1,0:T(8,128)S(1)}, f32[832,128]{1,0:T(8,128)S(1)}, u32[]{:S(2)}, u32[]{:S(2)}) collective-permute-start(f32[832,128]{1,0:T(8,128)S(1)} %pack_rest.1), channel_id=1, source_target_pairs={{0,2},{1,3},{4,6},{5,7},{8,10},{9,11},{12,14},{13,15},{16,18},{17,... | collective-permute-start | bytes 1277960 | tf_op jit(solution)/shard_map/ppermute | solution.py:355
  11.2 3.3 %collective-permute-start.2 = (f32[8,128]{1,0:T(8,128)S(1)}, f32[8,128]{1,0:T(8,128)S(1)}, u32[]{:S(2)}, u32[]{:S(2)}) collective-permute-start(f32[8,128]{1,0:T(8,128)S(1)} %get-tuple-element.46.before), channel_id=1, source_target_pairs={{0,1},{1,0},{2,3},{3,2},{4,5},{5,4},{6,7},{7,6},{8,9},{9,8},{10,11... | collective-permute-start | bytes 12296 | tf_op jit(solution)/shard_map/ppermute | solution.py:350
  11.3 9.3 %collective-permute-start.5 = (f32[4,128,128]{2,1,0:T(8,128)S(1)}, f32[4,128,128]{2,1,0:T(8,128)S(1)}, u32[]{:S(2)}, u32[]{:S(2)}) collective-permute-start(f32[4,128,128]{2,1,0:T(8,128)S(1)} %get-tuple-element.51), channel_id=1, source_target_pairs={{4,8},{8,4},{6,10},{10,6},{5,9},{9,5},{7,11},{11,7},{20,24},{24,20... | collective-permute-start | bytes 786440 | tf_op jit(solution)/shard_map/ppermute | solution.py:439
  14.5 7.2 %collective-permute-start.4 = (f32[4,128,128]{2,1,0:T(8,128)S(1)}, f32[4,128,128]{2,1,0:T(8,128)S(1)}, u32[]{:S(2)}, u32[]{:S(2)}) collective-permute-start(f32[4,128,128]{2,1,0:T(8,128)S(1)} %get-tuple-element.50), channel_id=1, source_target_pairs={{0,4},{4,0},{2,6},{6,2},{8,12},{12,8},{10,14},{14,10},{1,5},{5,1},... | collective-permute-start | bytes 786440 | tf_op jit(solution)/shard_map/ppermute | solution.py:439
  15.4 2.3 %collective-permute-start.3 = (f32[8,128]{1,0:T(8,128)S(1)}, f32[8,128]{1,0:T(8,128)S(1)}, u32[]{:S(2)}, u32[]{:S(2)}) collective-permute-start(f32[8,128]{1,0:T(8,128)S(1)} %get-tuple-element.48), channel_id=1, source_target_pairs={{0,1},{1,0},{2,3},{3,2},{4,5},{5,4},{6,7},{7,6},{8,9},{9,8},{10,11... | collective-permute-start | bytes 12296 | tf_op jit(solution)/shard_map/ppermute | solution.py:350
  22.5 2.4 %collective-permute-start.8 = (f32[832,128]{1,0:T(8,128)S(1)}, f32[832,128]{1,0:T(8,128)S(1)}, u32[]{:S(2)}, u32[]{:S(2)}) collective-permute-start(f32[832,128]{1,0:T(8,128)S(1)} %collective-permute-done.7.mine), channel_id=1, source_target_pairs={{0,1},{1,0},{2,3},{3,2},{4,5},{5,4},{6,7},{7,6},{8,9},{9,8},{10,11... | collective-permute-start | bytes 1277960 | tf_op jit(solution)/shard_map/ppermute | solution.py:350
  23.4 1.8 %collective-permute-start.6 = (f32[8,128]{1,0:T(8,128)S(1)}, f32[8,128]{1,0:T(8,128)S(1)}, u32[]{:S(2)}, u32[]{:S(2)}) collective-permute-start(f32[8,128]{1,0:T(8,128)S(1)} %corners.2), channel_id=1, source_target_pairs={{0,1},{1,0},{2,3},{3,2},{4,5},{5,4},{6,7},{7,6},{8,9},{9,8},{10,11... | collective-permute-start | bytes 12296 | tf_op jit(solution)/shard_map/ppermute | solution.py:350
  28.7 3.4 %collective-permute-start.9 = (f32[8,128]{1,0:T(8,128)S(1)}, f32[8,128]{1,0:T(8,128)S(1)}, u32[]{:S(2)}, u32[]{:S(2)}) collective-permute-start(f32[8,128]{1,0:T(8,128)S(1)} %get-tuple-element.64), channel_id=1, source_target_pairs={{0,1},{1,0},{2,3},{3,2},{4,5},{5,4},{6,7},{7,6},{8,9},{9,8},{10,11... | collective-permute-start | bytes 12296 | tf_op jit(solution)/shard_map/ppermute | solution.py:350
  29.0 12.2 %collective-permute-start.12 = (f32[4,128,128]{2,1,0:T(8,128)S(1)}, f32[4,128,128]{2,1,0:T(8,128)S(1)}, u32[]{:S(2)}, u32[]{:S(2)}) collective-permute-start(f32[4,128,128]{2,1,0:T(8,128)S(1)} %get-tuple-element.68), channel_id=1, source_target_pairs={{6,10},{10,6},{7,11},{11,7},{22,26},{26,22},{23,27},{27,23}} | collective-permute-start | bytes 786440 | tf_op jit(solution)/shard_map/ppermute | solution.py:439
  32.1 9.3 %collective-permute-start.11 = (f32[4,128,128]{2,1,0:T(8,128)S(1)}, f32[4,128,128]{2,1,0:T(8,128)S(1)}, u32[]{:S(2)}, u32[]{:S(2)}) collective-permute-start(f32[4,128,128]{2,1,0:T(8,128)S(1)} %get-tuple-element.67), channel_id=1, source_target_pairs={{2,6},{6,2},{10,14},{14,10},{3,7},{7,3},{11,15},{15,11},{18,22},{2... | collective-permute-start | bytes 786440 | tf_op jit(solution)/shard_map/ppermute | solution.py:439
  37.5 1.4 %collective-permute-start.10 = (f32[8,128]{1,0:T(8,128)S(1)}, f32[8,128]{1,0:T(8,128)S(1)}, u32[]{:S(2)}, u32[]{:S(2)}) collective-permute-start(f32[8,128]{1,0:T(8,128)S(1)} %get-tuple-element.65), channel_id=1, source_target_pairs={{0,1},{1,0},{2,3},{3,2},{4,5},{5,4},{6,7},{7,6},{8,9},{9,8},{10,11... | collective-permute-start | bytes 12296 | tf_op jit(solution)/shard_map/ppermute | solution.py:350
  41.4 2.2 %collective-permute-start.13 = (f32[8,128]{1,0:T(8,128)S(1)}, f32[8,128]{1,0:T(8,128)S(1)}, u32[]{:S(2)}, u32[]{:S(2)}) collective-permute-start(f32[8,128]{1,0:T(8,128)S(1)} %corners.3), channel_id=1, source_target_pairs={{0,1},{1,0},{2,3},{3,2},{4,5},{5,4},{6,7},{7,6},{8,9},{9,8},{10,11... | collective-permute-start | bytes 12296 | tf_op jit(solution)/shard_map/ppermute | solution.py:350

commit v2 on v1

--- a/solution.py
+++ b/solution.py
@@ -93,14 +93,26 @@
         copy.wait()
 
 
-def corner_kernel(halo_a, halo_b, *refs):
+def corner_kernel(count, *refs):
     out = refs[-1]
     first = first_core()
-    tiles, cols = halo_a.shape[:2]
-    for i, halo in enumerate((halo_a, halo_b)):
+    tiles = refs[0].shape[0]
+    cols = refs[0].shape[1]
+    out[...] = jnp.zeros_like(out)
+    for i in range(count):
         for tile in range(tiles):
-            side = jnp.where(first, halo[tile, cols - 1 : cols, :], halo[tile, 0:1, :])
+            side = jnp.where(first, refs[i][tile, cols - 1 : cols, :], refs[i][tile, 0:1, :])
             out[i * tiles + tile : i * tiles + tile + 1, :] = side
+
+
+def append_kernel(msg, edges, out):
+    even = even_strip()
+    tiles = msg.shape[0]
+    at = msg.shape[1] - 8
+    for tile in range(tiles):
+        out[tile, at : at + 1, :] = jnp.where(
+            even, edges[2 * tile + 1 : 2 * tile + 2, :], edges[2 * tile : 2 * tile + 1, :]
+        )
 
 
 def store_reduce(w_high, at, rows):
@@ -199,7 +211,9 @@
         edge[at : at + 1, :] = jnp.where(first, part[cols - 1 : cols, :], part[0:1, :])
         turned.append(part)
     if msgs:
-        msgs[0][tile] = jnp.where(even, turned[-1], turned[0])
+        msgs[0][tile, :cols, :] = jnp.where(even, turned[-1], turned[0])
+        if msgs[0].shape[1] > cols:
+            msgs[0][tile, cols:, :] = jnp.zeros((msgs[0].shape[1] - cols, cm), F32)
         msgs[1][tile] = jnp.where(even, turned[0], turned[-1])
 
 
@@ -252,8 +266,9 @@
     def row_and_side(tile, i):
         if i in (-1, rows):
             from_a = even if i == rows else jnp.logical_not(even)
-            side_a, side_b = corners[tile : tile + 1, :], corners[tiles + tile : tiles + tile + 1, :]
-            return jnp.where(from_a, halo_a[tile], halo_b[tile]), jnp.where(from_a, side_a, side_b)
+            side_b = corners[tile : tile + 1, :]
+            side_a = halo_a[tile, cols : cols + 1, :] if level else corners[tiles + tile : tiles + tile + 1, :]
+            return jnp.where(from_a, halo_a[tile, :cols, :], halo_b[tile]), jnp.where(from_a, side_a, side_b)
         if i in (0, rows - 1):
             j = 0 if i == 0 else 1
             return r_border[tile, j], edge_border[2 * tile + j : 2 * tile + j + 1, :]
@@ -292,7 +307,7 @@
             for j in range(count):
                 before = field_rows(x, kind, rows, tile, j)
                 new = jnp.maximum(before + branch[:, j * cols : (j + 1) * cols] + shift_out[...], 0.0)
-                after.append(jnp.where(keep, new, before))
+                after.append(jnp.where(keep, new, before) if level else new)
                 if last:
                     whole = outs[-1]
                     whole[tile, pl.ds(chosen[j], whole.shape[1] // rows, stride=rows), :] = after[j]
@@ -413,16 +428,17 @@
             rest_shapes, moved=4 * cm * (c + 9 * cm),
         )
 
-    def reduced_shapes(kind):
+    def reduced_shapes(kind, level):
+        room = 8 if level else 0
         count = 2 if kind == "border" else inner
         shapes = [near((tiles, count, cols, cm)), near((-(-tiles * count // 8) * 8, cm))]
-        return shapes + ([near((tiles, cols, cm))] * 2 if kind == "border" else [])
+        return shapes + ([near((tiles, cols + room, cm)), near((tiles, cols, cm))] if kind == "border" else [])
 
     def reduce_call(kind, level, weights, before):
         return call(
             functools.partial(reduce_kernel, kind, rows), "reduce_" + kind,
             [(held, VMEM)] + [(a, VMEM) for a in weights] + [(before, ANY)],
-            reduced_shapes(kind), flops=3 * cells * c * cm, moved=4 * cells * c // 2,
+            reduced_shapes(kind, 0), flops=3 * cells * c * cm, moved=4 * cells * c // 2,
         )
 
     def scratch(kind):
@@ -435,12 +451,17 @@
 
     def halos(msg_a, msg_b, swapped, level):
         axes = ("strip", "section")
-        msg_a, _ = lax.optimization_barrier((msg_a, swapped))
+        if level:
+            shape = near((tiles, cols + 8, cm))
+            (msg_a,) = call(append_kernel, "append", [(msg_a, VMEM), (swapped, VMEM)], [shape], aliases={0: 0})
+        else:
+            msg_a, _ = lax.optimization_barrier((msg_a, swapped))
         return lax.ppermute(msg_a, axes, pairs(0, level)), lax.ppermute(msg_b, axes, pairs(1, level))
 
-    def with_corners(halo, before):
-        args = [(a, VMEM) for a in halo] + [(a, ANY) for a in before]
-        (corners,) = call(corner_kernel, "corners", args, [near((2 * tiles, cm))])
+    def with_corners(halo, before, count):
+        args = [(a, VMEM) for a in halo[1::-1][:count]] + [(a, ANY) for a in before]
+        shape = near((-(-count * tiles // 8) * 8, cm))
+        (corners,) = call(functools.partial(corner_kernel, count), "corners", args, [shape])
         return halo + (swap(corners), corners)
 
     def block_call(kind, level, x, sent, weights, next_weights, before, halo=None):
@@ -458,7 +479,7 @@
         more, out_specs, aliases, held_out = scratch(kind), None, None, near((tiles, count, c, cols))
         if last:
             held_out = near(flat.shape)
-        outs = [held_out] + ([] if last else reduced_shapes(kind))
+        outs = [held_out] + ([] if last else reduced_shapes(kind, level + 1))
         if last and kind == "border":
             outs = [pltpu.HBM(flat.shape, F32), held_out]
             out_specs = [ANY, VMEM]
@@ -476,7 +497,7 @@
     own = prepare_own(border[1])
     inside = reduce_call("inner", 0, weights, border[1])
     sent = ((border[0], edges), (inside[0], swap(inside[1])))
-    halo = with_corners(halo, (own[4], sent[0][1], sent[1][1]))
+    halo = with_corners(halo, (own[4], sent[0][1], sent[1][1]), 2)
     x_border = x_inner = held
     for level in range(sections):
         last = level == sections - 1
@@ -487,7 +508,7 @@
         if last:
             (part,) = block_call("inner", level, x_inner, sent, rest_of, None, first)
             if level > 0:
-                halo = with_corners(halo, (part,))
+                halo = with_corners(halo, (inside[1],), 1)
             whole = block_call("border", level, x_border, sent, rest_of, None, part, halo)[0]
         else:
             weights = reduce_weights(level + 1)
@@ -496,7 +517,7 @@
             halo = halos(border[2], border[3], edges, level + 1)
             x_inner, *inside = block_call("inner", level, x_inner, sent, rest_of, weights, x_border)
             if level + 1 < sections - 1:
-                halo = with_corners(halo, (inside[1],))
+                halo = with_corners(halo, (inside[1],), 1)
     return whole.reshape(1, tiles, c, rows, cols)
 
 

time: 48.5 us -> 48.3 us (level)
  the two profiles are of different devices: /device:TPU:15 before, /device:TPU:3 now
where the time goes in v2:
time: 48.3 us; the launch traced here: 48 us
  Pallas kernels  20.9 us (43%)
  starting transfers between devices  18.3 us (38%)
  waiting for transfers between devices  8.5 us (18%)
    pallas_call x15, Pallas kernels, call(): pl.pallas_call(kernel, name=name, in_specs=[spec for _, spec in args], ou...  20.9 us
    ppermute x2, starting transfers between devices, halos(): lax.ppermute(msg_a, axes, pairs(0, level))  9.59 us
    ppermute x8, starting transfers between devices, swap(): return lax.ppermute(array, 'col', [(0, 1), (1, 0)])  4.8 us
    ppermute x8, waiting for transfers between devices, swap(): return lax.ppermute(array, 'col', [(0, 1), (1, 0)])  3.34 us
    ppermute x2, waiting for transfers between devices, halos(): lax.ppermute(msg_a, axes, pairs(0, level))  2.6 us
    ppermute x2, starting transfers between devices, from_section(): lax.ppermute(array, 'section', [(i, i + step) for i in range(sections - s...  2.57 us
    ppermute x2, waiting for transfers between devices, from_section(): lax.ppermute(array, 'section', [(i, i + step) for i in range(sections - s...  2.56 us
    ppermute x2, starting transfers between devices, halos(): lax.ppermute(msg_b, axes, pairs(1, level))  1.34 us
  transfers between devices with their start and end apart: 14, of which 7 were waited for; matrix products, arithmetic and copies ran while one was open for 0% of the time, Pallas kernels for 26%

profile of v2, /device:TPU:3, one launch (start us, length us, event | category | flops | bytes accessed | tf_op | source)
XLA Modules:
  0.0 48.0 jit_solution(9879813668020717889)
XLA Ops:
  0.0 1.0 %pack_first.1.before.first.refs_14_.refs_9_ = f32[72,512]{1,0:T(8,128)S(1)} custom-call(f32[1,128,512]{2,1,0:T(8,128)} %w_reduce.3, f32[1,2,128]{2,1,0:T(2,128)} %gain_mid.1, f32[1,2,128]{2,1,0:T(2,128)} %bias_mid.1, f32[1,512]{1,0:T(1,128)} %gain_out.1, f32[1,512]{1,0:T(1,128)} %bias_out.1), custom_call_target="tpu_custom_call" | custom-call | bytes 131072 | tf_op jit(solution)/shard_map/pack_first/pallas_call | solution.py:341
  1.0 1.3 %collective-permute-start = (f32[72,512]{1,0:T(8,128)S(1)}, f32[72,512]{1,0:T(8,128)S(1)}, u32[]{:S(2)}, u32[]{:S(2)}) collective-permute-start(f32[72,512]{1,0:T(8,128)S(1)} %pack_first.1.before.first.refs_14_.refs_9_), channel_id=1, source_target_pairs={{0,2},{1,3},{4,6},{5,7},{8,10},{9,11},{12,14},{13,15},{16,18},{17,... | collective-permute-start | bytes 442376 | tf_op jit(solution)/shard_map/ppermute | solution.py:370
  2.3 2.3 %fetch.1 = (f32[4,2048,128]{2,1,0:T(8,128)S(1)}, f32[128,512]{1,0:T(8,128)S(1)}) custom-call(f32[4,2048,128]{2,1,0:T(8,128)} %bitcast.2, f32[1,128,512]{2,1,0:T(8,128)} %w_reduce.3, f32[72,512]{1,0:T(8,128)S(1)} %pack_first.1.before.first.refs_14_.refs_9_), custom_call_target="tpu_custom_call" | custom-call | bytes 4194304 | tf_op jit(solution)/shard_map/fetch/pallas_call | solution.py:341
  4.5 1.0 %pack_rest.1 = f32[832,128]{1,0:T(8,128)S(1)} custom-call(f32[1,9,128,128]{3,2,1,0:T(8,128)} %w_spatial.3, f32[1,512,128]{2,1,0:T(8,128)} %w_expand.3, f32[128,512]{1,0:T(8,128)S(1)} %get-tuple-element.41.before.w_reduce), custom_call_target="tpu_custom_call" | custom-call | bytes 425984 | tf_op jit(solution)/shard_map/pack_rest/pallas_call | solution.py:341
  5.6 2.0 %collective-permute-done.mine = f32[72,512]{1,0:T(8,128)S(1)} collective-permute-done((f32[72,512]{1,0:T(8,128)S(1)}, f32[72,512]{1,0:T(8,128)S(1)}, u32[]{:S(2)}, u32[]{:S(2)}) %collective-permute-start) | collective-permute-done | bytes 147488 | tf_op jit(solution)/shard_map/ppermute | solution.py:370
  7.6 1.5 %collective-permute-start.1 = (f32[72,512]{1,0:T(8,128)S(1)}, f32[72,512]{1,0:T(8,128)S(1)}, u32[]{:S(2)}, u32[]{:S(2)}) collective-permute-start(f32[72,512]{1,0:T(8,128)S(1)} %collective-permute-done.mine), channel_id=1, source_target_pairs={{0,1},{1,0},{2,3},{3,2},{4,5},{5,4},{6,7},{7,6},{8,9},{9,8},{10,11... | collective-permute-start | bytes 442376 | tf_op jit(solution)/shard_map/ppermute | solution.py:365
  9.1 1.3 %collective-permute-start.7 = (f32[832,128]{1,0:T(8,128)S(1)}, f32[832,128]{1,0:T(8,128)S(1)}, u32[]{:S(2)}, u32[]{:S(2)}) collective-permute-start(f32[832,128]{1,0:T(8,128)S(1)} %pack_rest.1), channel_id=1, source_target_pairs={{0,2},{1,3},{4,6},{5,7},{8,10},{9,11},{12,14},{13,15},{16,18},{17,... | collective-permute-start | bytes 1277960 | tf_op jit(solution)/shard_map/ppermute | solution.py:370
  10.4 0.0 collective-permute-done.1.other
  10.4 0.1 prepare_reduce.1
  10.5 0.7 %reduce_border.1 = (f32[4,2,128,128]{3,2,1,0:T(8,128)S(1)}, f32[8,128]{1,0:T(8,128)S(1)}, f32[4,128,128]{2,1,0:T(8,128)S(1)}, f32[4,128,128]{2,1,0:T(8,128)S(1)}) custom-call(f32[4,2048,128]{2,1,0:T(8,128)S(1)} %get-tuple-element.39.x.refs_0_, bf16[256,512]{1,0:T(8,128)(2,1)S(1)} %get-tuple-element.42.w_reduce, ...), custom_call_target="tpu_custom_call" | custom-call | flops 402653184 | bytes 2097152 | tf_op jit(solution)/shard_map/reduce_border/pallas_call | solution.py:341
  11.2 0.1 collective-permute-start.2
  11.3 0.7 %collective-permute-start.5 = (f32[4,128,128]{2,1,0:T(8,128)S(1)}, f32[4,128,128]{2,1,0:T(8,128)S(1)}, u32[]{:S(2)}, u32[]{:S(2)}) collective-permute-start(f32[4,128,128]{2,1,0:T(8,128)S(1)} %get-tuple-element.50), channel_id=1, source_target_pairs={{4,8},{8,4},{6,10},{10,6},{5,9},{9,5},{7,11},{11,7},{20,24},{24,20... | collective-permute-start | bytes 786440 | tf_op jit(solution)/shard_map/ppermute | solution.py:459
  12.0 0.4 collective-permute-done.2.refs_3_
  12.5 3.5 %collective-permute-start.4 = (f32[4,128,128]{2,1,0:T(8,128)S(1)}, f32[4,128,128]{2,1,0:T(8,128)S(1)}, u32[]{:S(2)}, u32[]{:S(2)}) collective-permute-start(f32[4,128,128]{2,1,0:T(8,128)S(1)} %get-tuple-element.49), channel_id=1, source_target_pairs={{0,4},{4,0},{2,6},{6,2},{8,12},{12,8},{10,14},{14,10},{1,5},{5,1},... | collective-permute-start | bytes 786440 | tf_op jit(solution)/shard_map/ppermute | solution.py:459
  15.9 0.7 %reduce_inner.1 = (f32[4,2,128,128]{3,2,1,0:T(8,128)S(1)}, f32[8,128]{1,0:T(8,128)S(1)}) custom-call(f32[4,2048,128]{2,1,0:T(8,128)S(1)} %get-tuple-element.39.x.refs_0_, bf16[256,512]{1,0:T(8,128)(2,1)S(1)} %get-tuple-element.42.w_reduce, f32[8,512]{1,0:T(8,128)S(1)} %get-tuple-element.43.terms.refs_11_.refs_8_, f32[8,128]{1,0:T(8,128)S(1)} %get-tuple-element.45.before), custom_call_target="tpu_custom_call" | custom-call | flops 402653184 | bytes 2097152 | tf_op jit(solution)/shard_map/reduce_inner/pallas_call | solution.py:341
  16.6 1.1 %collective-permute-start.3 = (f32[8,128]{1,0:T(8,128)S(1)}, f32[8,128]{1,0:T(8,128)S(1)}, u32[]{:S(2)}, u32[]{:S(2)}) collective-permute-start(f32[8,128]{1,0:T(8,128)S(1)} %get-tuple-element.47), channel_id=1, source_target_pairs={{0,1},{1,0},{2,3},{3,2},{4,5},{5,4},{6,7},{7,6},{8,9},{9,8},{10,11... | collective-permute-start | bytes 12296 | tf_op jit(solution)/shard_map/ppermute | solution.py:365
  17.7 1.5 %prepare_own.1 = (bf16[256,512]{1,0:T(8,128)(2,1)S(1)}, bf16[1152,256]{1,0:T(8,128)(2,1)S(1)}, bf16[512,384]{1,0:T(8,128)(2,1)S(1)}, f32[512,128]{1,0:T(8,128)S(1)}, f32[8,512]{1,0:T(8,128)S(1)}) custom-call(f32[128,512]{1,0:T(8,128)S(1)} %get-tuple-element.41.before.w_reduce, f32[1,9,128,128]{3,2,1,0:T(8,128)} %w_spatial.3, f32[1,512,128]{2,1,0:T(8,128)} %w_expand.3, ...), custom_call_target="tpu_custom_call" | custom-call | bytes 1114112 | tf_op jit(solution)/shard_map/prepare_own/pallas_call | solution.py:341
  19.3 0.0 collective-permute-done.3.refs_4_
  19.3 0.0 collective-permute-done.5.refs_0_.refs_6_
  19.3 2.6 %collective-permute-done.4.refs_1_.refs_5_ = f32[4,128,128]{2,1,0:T(8,128)S(1)} collective-permute-done((f32[4,128,128]{2,1,0:T(8,128)S(1)}, f32[4,128,128]{2,1,0:T(8,128)S(1)}, u32[]{:S(2)}, u32[]{:S(2)}) %collective-permute-start.4) | collective-permute-done | bytes 262176 | tf_op jit(solution)/shard_map/ppermute | solution.py:459
  21.9 0.6 %collective-permute-done.7.mine = f32[832,128]{1,0:T(8,128)S(1)} collective-permute-done((f32[832,128]{1,0:T(8,128)S(1)}, f32[832,128]{1,0:T(8,128)S(1)}, u32[]{:S(2)}, u32[]{:S(2)}) %collective-permute-start.7) | collective-permute-done | bytes 426016 | tf_op jit(solution)/shard_map/ppermute | solution.py:370
  22.5 0.8 %collective-permute-start.8 = (f32[832,128]{1,0:T(8,128)S(1)}, f32[832,128]{1,0:T(8,128)S(1)}, u32[]{:S(2)}, u32[]{:S(2)}) collective-permute-start(f32[832,128]{1,0:T(8,128)S(1)} %collective-permute-done.7.mine), channel_id=1, source_target_pairs={{0,1},{1,0},{2,3},{3,2},{4,5},{5,4},{6,7},{7,6},{8,9},{9,8},{10,11... | collective-permute-start | bytes 1277960 | tf_op jit(solution)/shard_map/ppermute | solution.py:365
  23.3 0.1 collective-permute-start.6
  23.3 1.3 %collective-permute-done.8.other = f32[832,128]{1,0:T(8,128)S(1)} collective-permute-done((f32[832,128]{1,0:T(8,128)S(1)}, f32[832,128]{1,0:T(8,128)S(1)}, u32[]{:S(2)}, u32[]{:S(2)}) %collective-permute-start.8) | collective-permute-done | bytes 426016 | tf_op jit(solution)/shard_map/ppermute | solution.py:365
  24.7 0.4 prepare_rest.1
  25.1 0.0 collective-permute-done.6.refs_7_
  25.1 3.4 %block_border.2 = (f32[4,2,512,128]{3,2,1,0:T(8,128)S(1)}, f32[4,2,128,128]{3,2,1,0:T(8,128)S(1)}, f32[8,128]{1,0:T(8,128)S(1)}, f32[4,136,128]{2,1,0:T(8,128)S(1)}, f32[4,128,128]{2,1,0:T(8,128)S(1)}) custom-call(f32[4,2048,128]{2,1,0:T(8,128)S(1)} %get-tuple-element.39.x.refs_0_, f32[4,2,128,128]{3,2,1,0:T(8,128)S(1)} %get-tuple-element.44.refs_1_, ...), custom_call_target="tpu_custom_call" | custom-call | flops 1711276032 | bytes 4194304 | tf_op jit(solution)/shard_map/block_border/pallas_call | solution.py:341
  28.5 0.7 %collective-permute-start.12 = (f32[4,128,128]{2,1,0:T(8,128)S(1)}, f32[4,128,128]{2,1,0:T(8,128)S(1)}, u32[]{:S(2)}, u32[]{:S(2)}) collective-permute-start(f32[4,128,128]{2,1,0:T(8,128)S(1)} %get-tuple-element.66), channel_id=1, source_target_pairs={{6,10},{10,6},{7,11},{11,7},{22,26},{26,22},{23,27},{27,23}} | collective-permute-start | bytes 786440 | tf_op jit(solution)/shard_map/ppermute | solution.py:459
  29.2 0.4 collective-permute-start.9
  29.6 0.9 %collective-permute-done.9.edges.refs_3_ = f32[8,128]{1,0:T(8,128)S(1)} collective-permute-done((f32[8,128]{1,0:T(8,128)S(1)}, f32[8,128]{1,0:T(8,128)S(1)}, u32[]{:S(2)}, u32[]{:S(2)}) %collective-permute-start.9) | collective-permute-done | bytes 4128 | tf_op jit(solution)/shard_map/ppermute | solution.py:365
  30.5 6.1 %collective-permute-start.11 = (f32[4,136,128]{2,1,0:T(8,128)S(1)}, f32[4,136,128]{2,1,0:T(8,128)S(1)}, u32[]{:S(2)}, u32[]{:S(2)}) collective-permute-start(f32[4,136,128]{2,1,0:T(8,128)S(1)} %append.1), channel_id=1, source_target_pairs={{2,6},{6,2},{10,14},{14,10},{3,7},{7,3},{11,15},{15,11},{18,22},{2... | collective-permute-start | bytes 835592 | tf_op jit(solution)/shard_map/ppermute | solution.py:459
  36.6 3.4 %block_inner.2 = (f32[4,2,512,128]{3,2,1,0:T(8,128)S(1)}, f32[4,2,128,128]{3,2,1,0:T(8,128)S(1)}, f32[8,128]{1,0:T(8,128)S(1)}) custom-call(f32[4,2048,128]{2,1,0:T(8,128)S(1)} %get-tuple-element.39.x.refs_0_, f32[4,2,128,128]{3,2,1,0:T(8,128)S(1)} %get-tuple-element.44.refs_1_, f32[4,2,128,128]{3,2,1,0:T(8,128)S(1)} %get-tuple-element.46.refs_2_, ...), custom_call_target="tpu_custom_call" | custom-call | flops 1711276032 | bytes 4194304 | tf_op jit(solution)/shard_map/block_inner/pallas_call | solution.py:341
  39.9 0.7 %collective-permute-start.10 = (f32[8,128]{1,0:T(8,128)S(1)}, f32[8,128]{1,0:T(8,128)S(1)}, u32[]{:S(2)}, u32[]{:S(2)}) collective-permute-start(f32[8,128]{1,0:T(8,128)S(1)} %get-tuple-element.64.refs_1_), channel_id=1, source_target_pairs={{0,1},{1,0},{2,3},{3,2},{4,5},{5,4},{6,7},{7,6},{8,9},{9,8},{10,11... | collective-permute-start | bytes 12296 | tf_op jit(solution)/shard_map/ppermute | solution.py:365
  40.6 0.0 collective-permute-done.12.refs_0_.refs_6_
  40.6 0.1 collective-permute-start.13
  40.7 0.7 %collective-permute-done.10.refs_4_ = f32[8,128]{1,0:T(8,128)S(1)} collective-permute-done((f32[8,128]{1,0:T(8,128)S(1)}, f32[8,128]{1,0:T(8,128)S(1)}, u32[]{:S(2)}, u32[]{:S(2)}) %collective-permute-start.10) | collective-permute-done | bytes 4128 | tf_op jit(solution)/shard_map/ppermute | solution.py:365
  41.5 2.4 %block_inner.3.refs_12_ = f32[4,2048,128]{2,1,0:T(8,128)S(1)} custom-call(f32[4,2,512,128]{3,2,1,0:T(8,128)S(1)} %get-tuple-element.67.refs_0_, f32[4,2,128,128]{3,2,1,0:T(8,128)S(1)} %get-tuple-element.61.refs_1_, f32[4,2,128,128]{3,2,1,0:T(8,128)S(1)} %get-tuple-element.62.refs_2_, f32[8,128]{1,0:T(8,128)S(1)} %collective-permute-done.9.edges.refs_3_, ...), custom_call_target="tpu_custom_call" | custom-call | flops 1308622848 | bytes 4194304 | tf_op jit(solution)/shard_map/block_inner/pallas_call | solution.py:341
  43.8 0.0 collective-permute-done.13.refs_7_
  43.8 0.0 collective-permute-done.11.refs_5_
  43.9 4.0 %block_border.3 = (f32[4,2048,128]{2,1,0:T(8,128)}, f32[4,2048,128]{2,1,0:T(8,128)S(1)}) custom-call(f32[4,2,512,128]{3,2,1,0:T(8,128)S(1)} %get-tuple-element.60.refs_11_.refs_0_, f32[4,2,128,128]{3,2,1,0:T(8,128)S(1)} %get-tuple-element.61.refs_1_, f32[4,2,128,128]{3,2,1,0:T(8,128)S(1)} %get-tuple-element.62.refs_2_, ...), custom_call_target="tpu_custom_call", output_to_operand_aliasing={{1}: (12, {})} | custom-call | flops 1308622848 | bytes 4194304 | tf_op jit(solution)/shard_map/block_border/pallas_call | solution.py:341
  (3 shorter events, 0.0 us)
Async XLA Ops:
  1.0 6.6 %collective-permute-start = (f32[72,512]{1,0:T(8,128)S(1)}, f32[72,512]{1,0:T(8,128)S(1)}, u32[]{:S(2)}, u32[]{:S(2)}) collective-permute-start(f32[72,512]{1,0:T(8,128)S(1)} %pack_first.1.before.first.refs_14_.refs_9_), channel_id=1, source_target_pairs={{0,2},{1,3},{4,6},{5,7},{8,10},{9,11},{12,14},{13,15},{16,18},{17,... | collective-permute-start | bytes 442376 | tf_op jit(solution)/shard_map/ppermute | solution.py:370
  7.6 2.8 %collective-permute-start.1 = (f32[72,512]{1,0:T(8,128)S(1)}, f32[72,512]{1,0:T(8,128)S(1)}, u32[]{:S(2)}, u32[]{:S(2)}) collective-permute-start(f32[72,512]{1,0:T(8,128)S(1)} %collective-permute-done.mine), channel_id=1, source_target_pairs={{0,1},{1,0},{2,3},{3,2},{4,5},{5,4},{6,7},{7,6},{8,9},{9,8},{10,11... | collective-permute-start | bytes 442376 | tf_op jit(solution)/shard_map/ppermute | solution.py:365
  9.1 13.3 %collective-permute-start.7 = (f32[832,128]{1,0:T(8,128)S(1)}, f32[832,128]{1,0:T(8,128)S(1)}, u32[]{:S(2)}, u32[]{:S(2)}) collective-permute-start(f32[832,128]{1,0:T(8,128)S(1)} %pack_rest.1), channel_id=1, source_target_pairs={{0,2},{1,3},{4,6},{5,7},{8,10},{9,11},{12,14},{13,15},{16,18},{17,... | collective-permute-start | bytes 1277960 | tf_op jit(solution)/shard_map/ppermute | solution.py:370
  11.2 1.2 %collective-permute-start.2 = (f32[8,128]{1,0:T(8,128)S(1)}, f32[8,128]{1,0:T(8,128)S(1)}, u32[]{:S(2)}, u32[]{:S(2)}) collective-permute-start(f32[8,128]{1,0:T(8,128)S(1)} %get-tuple-element.45.before), channel_id=1, source_target_pairs={{0,1},{1,0},{2,3},{3,2},{4,5},{5,4},{6,7},{7,6},{8,9},{9,8},{10,11... | collective-permute-start | bytes 12296 | tf_op jit(solution)/shard_map/ppermute | solution.py:365
  11.3 7.9 %collective-permute-start.5 = (f32[4,128,128]{2,1,0:T(8,128)S(1)}, f32[4,128,128]{2,1,0:T(8,128)S(1)}, u32[]{:S(2)}, u32[]{:S(2)}) collective-permute-start(f32[4,128,128]{2,1,0:T(8,128)S(1)} %get-tuple-element.50), channel_id=1, source_target_pairs={{4,8},{8,4},{6,10},{10,6},{5,9},{9,5},{7,11},{11,7},{20,24},{24,20... | collective-permute-start | bytes 786440 | tf_op jit(solution)/shard_map/ppermute | solution.py:459
  12.5 9.4 %collective-permute-start.4 = (f32[4,128,128]{2,1,0:T(8,128)S(1)}, f32[4,128,128]{2,1,0:T(8,128)S(1)}, u32[]{:S(2)}, u32[]{:S(2)}) collective-permute-start(f32[4,128,128]{2,1,0:T(8,128)S(1)} %get-tuple-element.49), channel_id=1, source_target_pairs={{0,4},{4,0},{2,6},{6,2},{8,12},{12,8},{10,14},{14,10},{1,5},{5,1},... | collective-permute-start | bytes 786440 | tf_op jit(solution)/shard_map/ppermute | solution.py:459
  16.6 2.6 %collective-permute-start.3 = (f32[8,128]{1,0:T(8,128)S(1)}, f32[8,128]{1,0:T(8,128)S(1)}, u32[]{:S(2)}, u32[]{:S(2)}) collective-permute-start(f32[8,128]{1,0:T(8,128)S(1)} %get-tuple-element.47), channel_id=1, source_target_pairs={{0,1},{1,0},{2,3},{3,2},{4,5},{5,4},{6,7},{7,6},{8,9},{9,8},{10,11... | collective-permute-start | bytes 12296 | tf_op jit(solution)/shard_map/ppermute | solution.py:365
  22.5 2.2 %collective-permute-start.8 = (f32[832,128]{1,0:T(8,128)S(1)}, f32[832,128]{1,0:T(8,128)S(1)}, u32[]{:S(2)}, u32[]{:S(2)}) collective-permute-start(f32[832,128]{1,0:T(8,128)S(1)} %collective-permute-done.7.mine), channel_id=1, source_target_pairs={{0,1},{1,0},{2,3},{3,2},{4,5},{5,4},{6,7},{7,6},{8,9},{9,8},{10,11... | collective-permute-start | bytes 1277960 | tf_op jit(solution)/shard_map/ppermute | solution.py:365
  23.3 1.8 %collective-permute-start.6 = (f32[8,128]{1,0:T(8,128)S(1)}, f32[8,128]{1,0:T(8,128)S(1)}, u32[]{:S(2)}, u32[]{:S(2)}) collective-permute-start(f32[8,128]{1,0:T(8,128)S(1)} %corners.2), channel_id=1, source_target_pairs={{0,1},{1,0},{2,3},{3,2},{4,5},{5,4},{6,7},{7,6},{8,9},{9,8},{10,11... | collective-permute-start | bytes 12296 | tf_op jit(solution)/shard_map/ppermute | solution.py:365
  28.5 12.1 %collective-permute-start.12 = (f32[4,128,128]{2,1,0:T(8,128)S(1)}, f32[4,128,128]{2,1,0:T(8,128)S(1)}, u32[]{:S(2)}, u32[]{:S(2)}) collective-permute-start(f32[4,128,128]{2,1,0:T(8,128)S(1)} %get-tuple-element.66), channel_id=1, source_target_pairs={{6,10},{10,6},{7,11},{11,7},{22,26},{26,22},{23,27},{27,23}} | collective-permute-start | bytes 786440 | tf_op jit(solution)/shard_map/ppermute | solution.py:459
  29.2 1.2 %collective-permute-start.9 = (f32[8,128]{1,0:T(8,128)S(1)}, f32[8,128]{1,0:T(8,128)S(1)}, u32[]{:S(2)}, u32[]{:S(2)}) collective-permute-start(f32[8,128]{1,0:T(8,128)S(1)} %get-tuple-element.63), channel_id=1, source_target_pairs={{0,1},{1,0},{2,3},{3,2},{4,5},{5,4},{6,7},{7,6},{8,9},{9,8},{10,11... | collective-permute-start | bytes 12296 | tf_op jit(solution)/shard_map/ppermute | solution.py:365
  30.5 13.4 %collective-permute-start.11 = (f32[4,136,128]{2,1,0:T(8,128)S(1)}, f32[4,136,128]{2,1,0:T(8,128)S(1)}, u32[]{:S(2)}, u32[]{:S(2)}) collective-permute-start(f32[4,136,128]{2,1,0:T(8,128)S(1)} %append.1), channel_id=1, source_target_pairs={{2,6},{6,2},{10,14},{14,10},{3,7},{7,3},{11,15},{15,11},{18,22},{2... | collective-permute-start | bytes 835592 | tf_op jit(solution)/shard_map/ppermute | solution.py:459
  39.9 1.5 %collective-permute-start.10 = (f32[8,128]{1,0:T(8,128)S(1)}, f32[8,128]{1,0:T(8,128)S(1)}, u32[]{:S(2)}, u32[]{:S(2)}) collective-permute-start(f32[8,128]{1,0:T(8,128)S(1)} %get-tuple-element.64.refs_1_), channel_id=1, source_target_pairs={{0,1},{1,0},{2,3},{3,2},{4,5},{5,4},{6,7},{7,6},{8,9},{9,8},{10,11... | collective-permute-start | bytes 12296 | tf_op jit(solution)/shard_map/ppermute | solution.py:365
  40.6 3.2 %collective-permute-start.13 = (f32[8,128]{1,0:T(8,128)S(1)}, f32[8,128]{1,0:T(8,128)S(1)}, u32[]{:S(2)}, u32[]{:S(2)}) collective-permute-start(f32[8,128]{1,0:T(8,128)S(1)} %corners.3), channel_id=1, source_target_pairs={{0,1},{1,0},{2,3},{3,2},{4,5},{5,4},{6,7},{7,6},{8,9},{9,8},{10,11... | collective-permute-start | bytes 12296 | tf_op jit(solution)/shard_map/ppermute | solution.py:365

commit v3 on v2

--- a/solution.py
+++ b/solution.py
@@ -29,8 +29,8 @@
     return lax.axis_index("col") == 0
 
 
-def even_strip():
-    return lax.axis_index("strip") % 2 == 0
+def even_strip(level):
+    return lax.axis_index("strip") % 2 == (1 if level else 0)
 
 
 def column_of(row):
@@ -106,7 +106,7 @@
 
 
 def append_kernel(msg, edges, out):
-    even = even_strip()
+    even = even_strip(1)
     tiles = msg.shape[0]
     at = msg.shape[1] - 8
     for tile in range(tiles):
@@ -195,14 +195,14 @@
     return (0, rows - 1) if kind == "border" else tuple(range(1, rows - 1))
 
 
-def reduce_step(tile, field, w_reduce, terms, r_out, edge, msgs):
+def reduce_step(level, tile, field, w_reduce, terms, r_out, edge, msgs):
     cm = w_reduce.shape[0] // 2
     count, cols = r_out.shape[1:3]
     high, low = split(field)
     both = dot(w_reduce[...], high)
     total = both[:cm] + both[cm:] + dot(w_reduce[:cm, :], low)
     gain, shift = terms[0:1, 0:cm], terms[0:1, 2 * cm : 3 * cm]
-    even, first = even_strip(), first_core()
+    even, first = even_strip(level), first_core()
     turned = []
     for j in range(count):
         part = jnp.maximum(jnp.transpose(total[:, j * cols : (j + 1) * cols]) * gain + shift, 0.0)
@@ -228,7 +228,7 @@
     count = r_out.shape[1]
     for tile in range(x.shape[0]):
         field = jnp.concatenate([field_rows(x, kind, rows, tile, j) for j in range(count)], axis=1)
-        reduce_step(tile, field, w_reduce, terms, r_out, edge, msgs)
+        reduce_step(0, tile, field, w_reduce, terms, r_out, edge, msgs)
 
 
 def block_kernel(kind, rows, level, last, *refs):
@@ -259,7 +259,7 @@
     chosen = members(kind, rows)
     count = len(chosen)
     inner = members("inner", rows)
-    even, first = even_strip(), first_core()
+    even, first = even_strip(level), first_core()
     gain, shift = terms[0:1, cm : 2 * cm], terms[0:1, 3 * cm : 4 * cm]
     keep = lax.axis_index("section") >= level
 
@@ -315,7 +315,7 @@
                     outs[0][tile, j] = after[j]
             if not last:
                 field = jnp.concatenate(after, axis=1)
-                reduce_step(tile, field, next_reduce, next_terms, r_out, edge_out, msgs)
+                reduce_step(level + 1, tile, field, next_reduce, next_terms, r_out, edge_out, msgs)
             if last and border:
                 sem = refs[0]
                 pltpu.make_async_copy(outs[1].at[tile], outs[0].at[tile], sem.at[tile]).start()
@@ -456,7 +456,10 @@
             (msg_a,) = call(append_kernel, "append", [(msg_a, VMEM), (swapped, VMEM)], [shape], aliases={0: 0})
         else:
             msg_a, _ = lax.optimization_barrier((msg_a, swapped))
-        return lax.ppermute(msg_a, axes, pairs(0, level)), lax.ppermute(msg_b, axes, pairs(1, level))
+        return (
+            lax.ppermute(msg_a, axes, pairs(1 if level else 0, level)),
+            lax.ppermute(msg_b, axes, pairs(0 if level else 1, level)),
+        )
 
     def with_corners(halo, before, count):
         args = [(a, VMEM) for a in halo[1::-1][:count]] + [(a, ANY) for a in before]

time: 48.3 us -> 48.3 us (level)
  the two profiles are of different devices: /device:TPU:3 before, /device:TPU:15 now
where the time goes in v3:
time: 48.3 us; the launch traced here: 48 us
  Pallas kernels  20.9 us (43%)
  starting transfers between devices  17.2 us (36%)
  waiting for transfers between devices  9.6 us (20%)
    pallas_call x15, Pallas kernels, call(): pl.pallas_call(kernel, name=name, in_specs=[spec for _, spec in args], ou...  20.9 us
    ppermute x2, starting transfers between devices, halos(): lax.ppermute(msg_b, axes, pairs(0 if level else 1, level))  5.11 us
    ppermute x8, starting transfers between devices, swap(): return lax.ppermute(array, 'col', [(0, 1), (1, 0)])  4.96 us
    ppermute x2, starting transfers between devices, halos(): lax.ppermute(msg_a, axes, pairs(1 if level else 0, level))  4.55 us
    ppermute x2, waiting for transfers between devices, halos(): lax.ppermute(msg_b, axes, pairs(0 if level else 1, level))  2.94 us
    ppermute x8, waiting for transfers between devices, swap(): return lax.ppermute(array, 'col', [(0, 1), (1, 0)])  2.87 us
    ppermute x2, waiting for transfers between devices, from_section(): lax.ppermute(array, 'section', [(i, i + step) for i in range(sections - s...  2.72 us
    ppermute x2, starting transfers between devices, from_section(): lax.ppermute(array, 'section', [(i, i + step) for i in range(sections - s...  2.57 us
  transfers between devices with their start and end apart: 14, of which 7 were waited for; matrix products, arithmetic and copies ran while one was open for 0% of the time, Pallas kernels for 26%

profile of v3, /device:TPU:15, one launch (start us, length us, event | category | flops | bytes accessed | tf_op | source)
XLA Modules:
  0.0 48.0 jit_solution(12847500546915587765)
XLA Ops:
  0.0 1.0 %pack_first.1.before.first.refs_14_.refs_9_ = f32[72,512]{1,0:T(8,128)S(1)} custom-call(f32[1,128,512]{2,1,0:T(8,128)} %w_reduce.3, f32[1,2,128]{2,1,0:T(2,128)} %gain_mid.1, f32[1,2,128]{2,1,0:T(2,128)} %bias_mid.1, f32[1,512]{1,0:T(1,128)} %gain_out.1, f32[1,512]{1,0:T(1,128)} %bias_out.1), custom_call_target="tpu_custom_call" | custom-call | bytes 131072 | tf_op jit(solution)/shard_map/pack_first/pallas_call | solution.py:341
  1.0 1.3 %collective-permute-start = (f32[72,512]{1,0:T(8,128)S(1)}, f32[72,512]{1,0:T(8,128)S(1)}, u32[]{:S(2)}, u32[]{:S(2)}) collective-permute-start(f32[72,512]{1,0:T(8,128)S(1)} %pack_first.1.before.first.refs_14_.refs_9_), channel_id=1, source_target_pairs={{0,2},{1,3},{4,6},{5,7},{8,10},{9,11},{12,14},{13,15},{16,18},{17,... | collective-permute-start | bytes 442376 | tf_op jit(solution)/shard_map/ppermute | solution.py:370
  2.3 2.3 %fetch.1 = (f32[4,2048,128]{2,1,0:T(8,128)S(1)}, f32[128,512]{1,0:T(8,128)S(1)}) custom-call(f32[4,2048,128]{2,1,0:T(8,128)} %bitcast.2, f32[1,128,512]{2,1,0:T(8,128)} %w_reduce.3, f32[72,512]{1,0:T(8,128)S(1)} %pack_first.1.before.first.refs_14_.refs_9_), custom_call_target="tpu_custom_call" | custom-call | bytes 4194304 | tf_op jit(solution)/shard_map/fetch/pallas_call | solution.py:341
  4.5 1.0 %pack_rest.1 = f32[832,128]{1,0:T(8,128)S(1)} custom-call(f32[1,9,128,128]{3,2,1,0:T(8,128)} %w_spatial.3, f32[1,512,128]{2,1,0:T(8,128)} %w_expand.3, f32[128,512]{1,0:T(8,128)S(1)} %get-tuple-element.41.before.w_reduce), custom_call_target="tpu_custom_call" | custom-call | bytes 425984 | tf_op jit(solution)/shard_map/pack_rest/pallas_call | solution.py:341
  5.6 2.0 %collective-permute-done.mine = f32[72,512]{1,0:T(8,128)S(1)} collective-permute-done((f32[72,512]{1,0:T(8,128)S(1)}, f32[72,512]{1,0:T(8,128)S(1)}, u32[]{:S(2)}, u32[]{:S(2)}) %collective-permute-start) | collective-permute-done | bytes 147488 | tf_op jit(solution)/shard_map/ppermute | solution.py:370
  7.6 1.5 %collective-permute-start.1 = (f32[72,512]{1,0:T(8,128)S(1)}, f32[72,512]{1,0:T(8,128)S(1)}, u32[]{:S(2)}, u32[]{:S(2)}) collective-permute-start(f32[72,512]{1,0:T(8,128)S(1)} %collective-permute-done.mine), channel_id=1, source_target_pairs={{0,1},{1,0},{2,3},{3,2},{4,5},{5,4},{6,7},{7,6},{8,9},{9,8},{10,11... | collective-permute-start | bytes 442376 | tf_op jit(solution)/shard_map/ppermute | solution.py:365
  9.1 1.3 %collective-permute-start.7 = (f32[832,128]{1,0:T(8,128)S(1)}, f32[832,128]{1,0:T(8,128)S(1)}, u32[]{:S(2)}, u32[]{:S(2)}) collective-permute-start(f32[832,128]{1,0:T(8,128)S(1)} %pack_rest.1), channel_id=1, source_target_pairs={{0,2},{1,3},{4,6},{5,7},{8,10},{9,11},{12,14},{13,15},{16,18},{17,... | collective-permute-start | bytes 1277960 | tf_op jit(solution)/shard_map/ppermute | solution.py:370
  10.4 0.0 collective-permute-done.1.other
  10.4 0.1 prepare_reduce.1
  10.5 0.7 %reduce_border.1 = (f32[4,2,128,128]{3,2,1,0:T(8,128)S(1)}, f32[8,128]{1,0:T(8,128)S(1)}, f32[4,128,128]{2,1,0:T(8,128)S(1)}, f32[4,128,128]{2,1,0:T(8,128)S(1)}) custom-call(f32[4,2048,128]{2,1,0:T(8,128)S(1)} %get-tuple-element.39.x.refs_0_, bf16[256,512]{1,0:T(8,128)(2,1)S(1)} %get-tuple-element.42.w_reduce, ...), custom_call_target="tpu_custom_call" | custom-call | flops 402653184 | bytes 2097152 | tf_op jit(solution)/shard_map/reduce_border/pallas_call | solution.py:341
  11.2 0.1 collective-permute-start.2
  11.3 3.2 %collective-permute-start.5 = (f32[4,128,128]{2,1,0:T(8,128)S(1)}, f32[4,128,128]{2,1,0:T(8,128)S(1)}, u32[]{:S(2)}, u32[]{:S(2)}) collective-permute-start(f32[4,128,128]{2,1,0:T(8,128)S(1)} %get-tuple-element.50), channel_id=1, source_target_pairs={{4,8},{8,4},{6,10},{10,6},{5,9},{9,5},{7,11},{11,7},{20,24},{24,20... | collective-permute-start | bytes 786440 | tf_op jit(solution)/shard_map/ppermute | solution.py:461
  14.5 0.0 collective-permute-done.2.refs_3_
  14.5 0.1 collective-permute-start.4
  14.6 0.7 %reduce_inner.1 = (f32[4,2,128,128]{3,2,1,0:T(8,128)S(1)}, f32[8,128]{1,0:T(8,128)S(1)}) custom-call(f32[4,2048,128]{2,1,0:T(8,128)S(1)} %get-tuple-element.39.x.refs_0_, bf16[256,512]{1,0:T(8,128)(2,1)S(1)} %get-tuple-element.42.w_reduce, f32[8,512]{1,0:T(8,128)S(1)} %get-tuple-element.43.terms.refs_11_.refs_8_, f32[8,128]{1,0:T(8,128)S(1)} %get-tuple-element.45.before), custom_call_target="tpu_custom_call" | custom-call | flops 402653184 | bytes 2097152 | tf_op jit(solution)/shard_map/reduce_inner/pallas_call | solution.py:341
  15.4 0.8 %collective-permute-start.3 = (f32[8,128]{1,0:T(8,128)S(1)}, f32[8,128]{1,0:T(8,128)S(1)}, u32[]{:S(2)}, u32[]{:S(2)}) collective-permute-start(f32[8,128]{1,0:T(8,128)S(1)} %get-tuple-element.47), channel_id=1, source_target_pairs={{0,1},{1,0},{2,3},{3,2},{4,5},{5,4},{6,7},{7,6},{8,9},{9,8},{10,11... | collective-permute-start | bytes 12296 | tf_op jit(solution)/shard_map/ppermute | solution.py:365
  16.2 1.5 %prepare_own.1 = (bf16[256,512]{1,0:T(8,128)(2,1)S(1)}, bf16[1152,256]{1,0:T(8,128)(2,1)S(1)}, bf16[512,384]{1,0:T(8,128)(2,1)S(1)}, f32[512,128]{1,0:T(8,128)S(1)}, f32[8,512]{1,0:T(8,128)S(1)}) custom-call(f32[128,512]{1,0:T(8,128)S(1)} %get-tuple-element.41.before.w_reduce, f32[1,9,128,128]{3,2,1,0:T(8,128)} %w_spatial.3, f32[1,512,128]{2,1,0:T(8,128)} %w_expand.3, ...), custom_call_target="tpu_custom_call" | custom-call | bytes 1114112 | tf_op jit(solution)/shard_map/prepare_own/pallas_call | solution.py:341
  17.7 0.0 collective-permute-done.3.refs_4_
  17.7 2.9 %collective-permute-done.5.refs_0_.refs_6_ = f32[4,128,128]{2,1,0:T(8,128)S(1)} collective-permute-done((f32[4,128,128]{2,1,0:T(8,128)S(1)}, f32[4,128,128]{2,1,0:T(8,128)S(1)}, u32[]{:S(2)}, u32[]{:S(2)}) %collective-permute-start.5) | collective-permute-done | bytes 262176 | tf_op jit(solution)/shard_map/ppermute | solution.py:461
  20.6 1.1 %collective-permute-done.4.refs_1_.refs_5_ = f32[4,128,128]{2,1,0:T(8,128)S(1)} collective-permute-done((f32[4,128,128]{2,1,0:T(8,128)S(1)}, f32[4,128,128]{2,1,0:T(8,128)S(1)}, u32[]{:S(2)}, u32[]{:S(2)}) %collective-permute-start.4) | collective-permute-done | bytes 262176 | tf_op jit(solution)/shard_map/ppermute | solution.py:460
  21.7 0.7 %collective-permute-done.7.mine = f32[832,128]{1,0:T(8,128)S(1)} collective-permute-done((f32[832,128]{1,0:T(8,128)S(1)}, f32[832,128]{1,0:T(8,128)S(1)}, u32[]{:S(2)}, u32[]{:S(2)}) %collective-permute-start.7) | collective-permute-done | bytes 426016 | tf_op jit(solution)/shard_map/ppermute | solution.py:370
  22.5 1.0 %collective-permute-start.8 = (f32[832,128]{1,0:T(8,128)S(1)}, f32[832,128]{1,0:T(8,128)S(1)}, u32[]{:S(2)}, u32[]{:S(2)}) collective-permute-start(f32[832,128]{1,0:T(8,128)S(1)} %collective-permute-done.7.mine), channel_id=1, source_target_pairs={{0,1},{1,0},{2,3},{3,2},{4,5},{5,4},{6,7},{7,6},{8,9},{9,8},{10,11... | collective-permute-start | bytes 1277960 | tf_op jit(solution)/shard_map/ppermute | solution.py:365
  23.4 0.1 collective-permute-start.6
  23.5 1.3 %collective-permute-done.8.other = f32[832,128]{1,0:T(8,128)S(1)} collective-permute-done((f32[832,128]{1,0:T(8,128)S(1)}, f32[832,128]{1,0:T(8,128)S(1)}, u32[]{:S(2)}, u32[]{:S(2)}) %collective-permute-start.8) | collective-permute-done | bytes 426016 | tf_op jit(solution)/shard_map/ppermute | solution.py:365
  24.8 0.4 prepare_rest.1
  25.3 0.0 collective-permute-done.6.refs_7_
  25.3 3.4 %block_border.2 = (f32[4,2,512,128]{3,2,1,0:T(8,128)S(1)}, f32[4,2,128,128]{3,2,1,0:T(8,128)S(1)}, f32[8,128]{1,0:T(8,128)S(1)}, f32[4,136,128]{2,1,0:T(8,128)S(1)}, f32[4,128,128]{2,1,0:T(8,128)S(1)}) custom-call(f32[4,2048,128]{2,1,0:T(8,128)S(1)} %get-tuple-element.39.x.refs_0_, f32[4,2,128,128]{3,2,1,0:T(8,128)S(1)} %get-tuple-element.44.refs_1_, ...), custom_call_target="tpu_custom_call" | custom-call | flops 1711276032 | bytes 4194304 | tf_op jit(solution)/shard_map/block_border/pallas_call | solution.py:341
  28.7 1.9 %collective-permute-start.12 = (f32[4,128,128]{2,1,0:T(8,128)S(1)}, f32[4,128,128]{2,1,0:T(8,128)S(1)}, u32[]{:S(2)}, u32[]{:S(2)}) collective-permute-start(f32[4,128,128]{2,1,0:T(8,128)S(1)} %get-tuple-element.66), channel_id=1, source_target_pairs={{2,6},{6,2},{10,14},{14,10},{3,7},{7,3},{11,15},{15,11},{18,22},{2... | collective-permute-start | bytes 786440 | tf_op jit(solution)/shard_map/ppermute | solution.py:461
  30.6 0.7 %collective-permute-start.9 = (f32[8,128]{1,0:T(8,128)S(1)}, f32[8,128]{1,0:T(8,128)S(1)}, u32[]{:S(2)}, u32[]{:S(2)}) collective-permute-start(f32[8,128]{1,0:T(8,128)S(1)} %get-tuple-element.63), channel_id=1, source_target_pairs={{0,1},{1,0},{2,3},{3,2},{4,5},{5,4},{6,7},{7,6},{8,9},{9,8},{10,11... | collective-permute-start | bytes 12296 | tf_op jit(solution)/shard_map/ppermute | solution.py:365
  31.3 0.8 %collective-permute-done.9.edges.refs_3_ = f32[8,128]{1,0:T(8,128)S(1)} collective-permute-done((f32[8,128]{1,0:T(8,128)S(1)}, f32[8,128]{1,0:T(8,128)S(1)}, u32[]{:S(2)}, u32[]{:S(2)}) %collective-permute-start.9) | collective-permute-done | bytes 4128 | tf_op jit(solution)/shard_map/ppermute | solution.py:365
  32.1 4.5 %collective-permute-start.11 = (f32[4,136,128]{2,1,0:T(8,128)S(1)}, f32[4,136,128]{2,1,0:T(8,128)S(1)}, u32[]{:S(2)}, u32[]{:S(2)}) collective-permute-start(f32[4,136,128]{2,1,0:T(8,128)S(1)} %append.1), channel_id=1, source_target_pairs={{6,10},{10,6},{7,11},{11,7},{22,26},{26,22},{23,27},{27,23}} | collective-permute-start | bytes 835592 | tf_op jit(solution)/shard_map/ppermute | solution.py:460
  36.6 3.4 %block_inner.2 = (f32[4,2,512,128]{3,2,1,0:T(8,128)S(1)}, f32[4,2,128,128]{3,2,1,0:T(8,128)S(1)}, f32[8,128]{1,0:T(8,128)S(1)}) custom-call(f32[4,2048,128]{2,1,0:T(8,128)S(1)} %get-tuple-element.39.x.refs_0_, f32[4,2,128,128]{3,2,1,0:T(8,128)S(1)} %get-tuple-element.44.refs_1_, f32[4,2,128,128]{3,2,1,0:T(8,128)S(1)} %get-tuple-element.46.refs_2_, ...), custom_call_target="tpu_custom_call" | custom-call | flops 1711276032 | bytes 4194304 | tf_op jit(solution)/shard_map/block_inner/pallas_call | solution.py:341
  40.0 0.7 %collective-permute-start.10 = (f32[8,128]{1,0:T(8,128)S(1)}, f32[8,128]{1,0:T(8,128)S(1)}, u32[]{:S(2)}, u32[]{:S(2)}) collective-permute-start(f32[8,128]{1,0:T(8,128)S(1)} %get-tuple-element.64.refs_1_), channel_id=1, source_target_pairs={{0,1},{1,0},{2,3},{3,2},{4,5},{5,4},{6,7},{7,6},{8,9},{9,8},{10,11... | collective-permute-start | bytes 12296 | tf_op jit(solution)/shard_map/ppermute | solution.py:365
  40.6 0.0 collective-permute-done.12.refs_0_.refs_6_
  40.7 0.1 collective-permute-start.13
  40.8 0.7 %collective-permute-done.10.refs_4_ = f32[8,128]{1,0:T(8,128)S(1)} collective-permute-done((f32[8,128]{1,0:T(8,128)S(1)}, f32[8,128]{1,0:T(8,128)S(1)}, u32[]{:S(2)}, u32[]{:S(2)}) %collective-permute-start.10) | collective-permute-done | bytes 4128 | tf_op jit(solution)/shard_map/ppermute | solution.py:365
  41.5 2.4 %block_inner.3.refs_12_ = f32[4,2048,128]{2,1,0:T(8,128)S(1)} custom-call(f32[4,2,512,128]{3,2,1,0:T(8,128)S(1)} %get-tuple-element.67.refs_0_, f32[4,2,128,128]{3,2,1,0:T(8,128)S(1)} %get-tuple-element.61.refs_1_, f32[4,2,128,128]{3,2,1,0:T(8,128)S(1)} %get-tuple-element.62.refs_2_, f32[8,128]{1,0:T(8,128)S(1)} %collective-permute-done.9.edges.refs_3_, ...), custom_call_target="tpu_custom_call" | custom-call | flops 1308622848 | bytes 4194304 | tf_op jit(solution)/shard_map/block_inner/pallas_call | solution.py:341
  43.8 0.0 collective-permute-done.13.refs_7_
  43.9 0.0 collective-permute-done.11.refs_5_
  43.9 4.0 %block_border.3 = (f32[4,2048,128]{2,1,0:T(8,128)}, f32[4,2048,128]{2,1,0:T(8,128)S(1)}) custom-call(f32[4,2,512,128]{3,2,1,0:T(8,128)S(1)} %get-tuple-element.60.refs_11_.refs_0_, f32[4,2,128,128]{3,2,1,0:T(8,128)S(1)} %get-tuple-element.61.refs_1_, f32[4,2,128,128]{3,2,1,0:T(8,128)S(1)} %get-tuple-element.62.refs_2_, ...), custom_call_target="tpu_custom_call", output_to_operand_aliasing={{1}: (12, {})} | custom-call | flops 1308622848 | bytes 4194304 | tf_op jit(solution)/shard_map/block_border/pallas_call | solution.py:341
  (3 shorter events, 0.0 us)
Async XLA Ops:
  1.0 6.6 %collective-permute-start = (f32[72,512]{1,0:T(8,128)S(1)}, f32[72,512]{1,0:T(8,128)S(1)}, u32[]{:S(2)}, u32[]{:S(2)}) collective-permute-start(f32[72,512]{1,0:T(8,128)S(1)} %pack_first.1.before.first.refs_14_.refs_9_), channel_id=1, source_target_pairs={{0,2},{1,3},{4,6},{5,7},{8,10},{9,11},{12,14},{13,15},{16,18},{17,... | collective-permute-start | bytes 442376 | tf_op jit(solution)/shard_map/ppermute | solution.py:370
  7.6 2.8 %collective-permute-start.1 = (f32[72,512]{1,0:T(8,128)S(1)}, f32[72,512]{1,0:T(8,128)S(1)}, u32[]{:S(2)}, u32[]{:S(2)}) collective-permute-start(f32[72,512]{1,0:T(8,128)S(1)} %collective-permute-done.mine), channel_id=1, source_target_pairs={{0,1},{1,0},{2,3},{3,2},{4,5},{5,4},{6,7},{7,6},{8,9},{9,8},{10,11... | collective-permute-start | bytes 442376 | tf_op jit(solution)/shard_map/ppermute | solution.py:365
  9.1 13.3 %collective-permute-start.7 = (f32[832,128]{1,0:T(8,128)S(1)}, f32[832,128]{1,0:T(8,128)S(1)}, u32[]{:S(2)}, u32[]{:S(2)}) collective-permute-start(f32[832,128]{1,0:T(8,128)S(1)} %pack_rest.1), channel_id=1, source_target_pairs={{0,2},{1,3},{4,6},{5,7},{8,10},{9,11},{12,14},{13,15},{16,18},{17,... | collective-permute-start | bytes 1277960 | tf_op jit(solution)/shard_map/ppermute | solution.py:370
  11.2 3.3 %collective-permute-start.2 = (f32[8,128]{1,0:T(8,128)S(1)}, f32[8,128]{1,0:T(8,128)S(1)}, u32[]{:S(2)}, u32[]{:S(2)}) collective-permute-start(f32[8,128]{1,0:T(8,128)S(1)} %get-tuple-element.45.before), channel_id=1, source_target_pairs={{0,1},{1,0},{2,3},{3,2},{4,5},{5,4},{6,7},{7,6},{8,9},{9,8},{10,11... | collective-permute-start | bytes 12296 | tf_op jit(solution)/shard_map/ppermute | solution.py:365
  11.3 9.3 %collective-permute-start.5 = (f32[4,128,128]{2,1,0:T(8,128)S(1)}, f32[4,128,128]{2,1,0:T(8,128)S(1)}, u32[]{:S(2)}, u32[]{:S(2)}) collective-permute-start(f32[4,128,128]{2,1,0:T(8,128)S(1)} %get-tuple-element.50), channel_id=1, source_target_pairs={{4,8},{8,4},{6,10},{10,6},{5,9},{9,5},{7,11},{11,7},{20,24},{24,20... | collective-permute-start | bytes 786440 | tf_op jit(solution)/shard_map/ppermute | solution.py:461
  14.5 7.2 %collective-permute-start.4 = (f32[4,128,128]{2,1,0:T(8,128)S(1)}, f32[4,128,128]{2,1,0:T(8,128)S(1)}, u32[]{:S(2)}, u32[]{:S(2)}) collective-permute-start(f32[4,128,128]{2,1,0:T(8,128)S(1)} %get-tuple-element.49), channel_id=1, source_target_pairs={{0,4},{4,0},{2,6},{6,2},{8,12},{12,8},{10,14},{14,10},{1,5},{5,1},... | collective-permute-start | bytes 786440 | tf_op jit(solution)/shard_map/ppermute | solution.py:460
  15.4 2.3 %collective-permute-start.3 = (f32[8,128]{1,0:T(8,128)S(1)}, f32[8,128]{1,0:T(8,128)S(1)}, u32[]{:S(2)}, u32[]{:S(2)}) collective-permute-start(f32[8,128]{1,0:T(8,128)S(1)} %get-tuple-element.47), channel_id=1, source_target_pairs={{0,1},{1,0},{2,3},{3,2},{4,5},{5,4},{6,7},{7,6},{8,9},{9,8},{10,11... | collective-permute-start | bytes 12296 | tf_op jit(solution)/shard_map/ppermute | solution.py:365
  22.5 2.4 %collective-permute-start.8 = (f32[832,128]{1,0:T(8,128)S(1)}, f32[832,128]{1,0:T(8,128)S(1)}, u32[]{:S(2)}, u32[]{:S(2)}) collective-permute-start(f32[832,128]{1,0:T(8,128)S(1)} %collective-permute-done.7.mine), channel_id=1, source_target_pairs={{0,1},{1,0},{2,3},{3,2},{4,5},{5,4},{6,7},{7,6},{8,9},{9,8},{10,11... | collective-permute-start | bytes 1277960 | tf_op jit(solution)/shard_map/ppermute | solution.py:365
  23.4 1.8 %collective-permute-start.6 = (f32[8,128]{1,0:T(8,128)S(1)}, f32[8,128]{1,0:T(8,128)S(1)}, u32[]{:S(2)}, u32[]{:S(2)}) collective-permute-start(f32[8,128]{1,0:T(8,128)S(1)} %corners.2), channel_id=1, source_target_pairs={{0,1},{1,0},{2,3},{3,2},{4,5},{5,4},{6,7},{7,6},{8,9},{9,8},{10,11... | collective-permute-start | bytes 12296 | tf_op jit(solution)/shard_map/ppermute | solution.py:365
  28.7 11.9 %collective-permute-start.12 = (f32[4,128,128]{2,1,0:T(8,128)S(1)}, f32[4,128,128]{2,1,0:T(8,128)S(1)}, u32[]{:S(2)}, u32[]{:S(2)}) collective-permute-start(f32[4,128,128]{2,1,0:T(8,128)S(1)} %get-tuple-element.66), channel_id=1, source_target_pairs={{2,6},{6,2},{10,14},{14,10},{3,7},{7,3},{11,15},{15,11},{18,22},{2... | collective-permute-start | bytes 786440 | tf_op jit(solution)/shard_map/ppermute | solution.py:461
  30.6 1.5 %collective-permute-start.9 = (f32[8,128]{1,0:T(8,128)S(1)}, f32[8,128]{1,0:T(8,128)S(1)}, u32[]{:S(2)}, u32[]{:S(2)}) collective-permute-start(f32[8,128]{1,0:T(8,128)S(1)} %get-tuple-element.63), channel_id=1, source_target_pairs={{0,1},{1,0},{2,3},{3,2},{4,5},{5,4},{6,7},{7,6},{8,9},{9,8},{10,11... | collective-permute-start | bytes 12296 | tf_op jit(solution)/shard_map/ppermute | solution.py:365
  32.1 11.7 %collective-permute-start.11 = (f32[4,136,128]{2,1,0:T(8,128)S(1)}, f32[4,136,128]{2,1,0:T(8,128)S(1)}, u32[]{:S(2)}, u32[]{:S(2)}) collective-permute-start(f32[4,136,128]{2,1,0:T(8,128)S(1)} %append.1), channel_id=1, source_target_pairs={{6,10},{10,6},{7,11},{11,7},{22,26},{26,22},{23,27},{27,23}} | collective-permute-start | bytes 835592 | tf_op jit(solution)/shard_map/ppermute | solution.py:460
  40.0 1.5 %collective-permute-start.10 = (f32[8,128]{1,0:T(8,128)S(1)}, f32[8,128]{1,0:T(8,128)S(1)}, u32[]{:S(2)}, u32[]{:S(2)}) collective-permute-start(f32[8,128]{1,0:T(8,128)S(1)} %get-tuple-element.64.refs_1_), channel_id=1, source_target_pairs={{0,1},{1,0},{2,3},{3,2},{4,5},{5,4},{6,7},{7,6},{8,9},{9,8},{10,11... | collective-permute-start | bytes 12296 | tf_op jit(solution)/shard_map/ppermute | solution.py:365
  40.7 3.2 %collective-permute-start.13 = (f32[8,128]{1,0:T(8,128)S(1)}, f32[8,128]{1,0:T(8,128)S(1)}, u32[]{:S(2)}, u32[]{:S(2)}) collective-permute-start(f32[8,128]{1,0:T(8,128)S(1)} %corners.3), channel_id=1, source_target_pairs={{0,1},{1,0},{2,3},{3,2},{4,5},{5,4},{6,7},{7,6},{8,9},{9,8},{10,11... | collective-permute-start | bytes 12296 | tf_op jit(solution)/shard_map/ppermute | solution.py:365
